TPU v7x, 32 devices: a whole 2x2x4 slice. The times are simulated.
32 devices in a mesh: section: 2 (over core), dp: 16 (over z, y, x).
Axes of the slice: x: 2, y: 2, z: 4, core: 2. Of those that a mesh axis runs over, the one named last changes fastest.
Arguments:
- inputs: bfloat16 [2, 32, 1024, 512], P('section', 'dp'), may hold values from -6 to 6
- lengths: int32 [2, 32], P('section', 'dp'), may hold values from 512 to 1024, as said below
- cotangent: bfloat16 [32, 1024, 512], P('dp'), may hold values from -6 to 6
- qkv_weight: bfloat16 [2, 512, 1536], P('section'), may hold values from -0.25 to 0.25
- out_weight: bfloat16 [2, 512, 512], P('section'), may hold values from -4 to 4
- cross_weight: bfloat16 [2, 512, 1024], P('section'), may hold values from -2.1283914 to 2.1283914
- ffn_in: bfloat16 [2, 512, 2048], P('section'), may hold values from -0.25 to 0.25
- ffn_out: bfloat16 [2, 2048, 512], P('section'), may hold values from -0.125 to 0.125
- norm_gain: float32 [2, 2, 512], P('section'), may hold values from 0.5 to 1.5
- norm_bias: float32 [2, 2, 512], P('section'), may hold values from -1.5 to 1.5
- cross_norm: float32 [2, 512], replicated, may hold values from -1.5 to 1.5
Outputs:
- layer_out: float32 [2, 32, 1024, 512], P('section', 'dp')
- input_grad: float32 [2, 32, 1024, 512], P('section', 'dp')
- qkv_grad: float32 [2, 512, 1536], P('section')
- out_grad: float32 [2, 512, 512], P('section')
- cross_grad: float32 [2, 512, 1024], P('section')
- ffn_in_grad: float32 [2, 512, 2048], P('section')
- ffn_out_grad: float32 [2, 2048, 512], P('section')
- gain_grad: float32 [2, 2, 512], P('section')
- bias_grad: float32 [2, 2, 512], P('section')
- cross_norm_grad: float32 [2, 512], P('section')
Inputs may be any that keep to these rules, and one draw needn't show every extreme that they name: `lengths`: the live slots of a sequence come first. In each of the two rows one sequence fills all 1024 slots.
All inputs are finite; a program needn't handle non-finite values.
Results may differ from a plain program's by a relative error of at most 0.018.
Values may be sent and summed in bfloat16 or wider, within the bound.
No kernel may reach another device: no remote copies, remote signals or barrier semaphores. Data moves between devices by JAX's collectives and lax.ppermute only.
A program may use at most 256 MiB of HBM per device.

v0:
```python
from functools import partial
import math

import jax
import jax.numpy as jnp
from jax import lax
from jax.sharding import PartitionSpec as P

HEAD_DIM = 64


def passed_along(block, axis, distance):
    devices = range(lax.axis_size(axis))
    route = [(i - distance, i) for i in devices if i - distance in devices]
    return lax.ppermute(block, axis, route)


def product(left_side, right_side):
    return jnp.dot(left_side, right_side, preferred_element_type=jnp.float32)


def product_tn(left_side, right_side):
    return lax.dot_general(
        left_side, right_side, (((0,), (0,)), ((), ())), preferred_element_type=jnp.float32
    )


def product_nt(left_side, right_side):
    return lax.dot_general(
        left_side, right_side, (((1,), (1,)), ((), ())), preferred_element_type=jnp.float32
    )


def tree_add(first_tree, second_tree):
    return jax.tree.map(jnp.add, first_tree, second_tree)


def tree_pick(condition, first_tree, second_tree):
    return jax.tree.map(partial(jnp.where, condition), first_tree, second_tree)


def zeros_wide(array_in):
    return jnp.zeros(array_in.shape, jnp.float32)


def norm_forward(field_in, gain_row, bias_row):
    centred = field_in - jnp.mean(field_in, -1, keepdims=True)
    inverse = lax.rsqrt(jnp.mean(centred * centred, -1, keepdims=True) + 1e-05)
    normed = centred * inverse
    return (normed * gain_row + bias_row, (normed, inverse))


def norm_backward(grad_rows, stored, gain_row):
    normed, inverse = stored
    scaled = grad_rows * gain_row
    inner = (
        scaled
        - jnp.mean(scaled, -1, keepdims=True)
        - normed * jnp.mean(scaled * normed, -1, keepdims=True)
    )
    return (inner * inverse, jnp.sum(grad_rows * normed, 0), jnp.sum(grad_rows, 0))


def gate_slope(raised):
    cumulative = 0.5 * (1.0 + lax.erf(raised * (1.0 / math.sqrt(2.0))))
    density = jnp.exp(-0.5 * raised * raised) * (1.0 / math.sqrt(2.0 * math.pi))
    return cumulative + raised * density


def split_heads(matrix):
    return matrix.reshape(matrix.shape[0], -1, HEAD_DIM)


def query_blocks(matrix):
    total_rows = matrix.shape[0]
    block_rows = min(512, total_rows)
    blocked = matrix.reshape(total_rows // block_rows, block_rows, -1, HEAD_DIM)
    return (blocked, jnp.arange(total_rows // block_rows, dtype=jnp.int32) * block_rows)


def masked_scores(query_part, key_heads, start_row, key_limit, causal):
    raw_scores = jnp.einsum(
        "qhd,khd->hqk", query_part, key_heads, preferred_element_type=jnp.float32
    )
    raw_scores = raw_scores * (1.0 / math.sqrt(HEAD_DIM))
    shape_pair = (query_part.shape[0], key_heads.shape[0])
    key_pos = lax.broadcasted_iota(jnp.int32, shape_pair, 1)
    allowed = key_pos < key_limit
    if causal:
        query_pos = start_row + lax.broadcasted_iota(jnp.int32, shape_pair, 0)
        allowed = jnp.logical_and(allowed, key_pos <= query_pos)
    return jnp.where(allowed[None], raw_scores, -1e30)


def attend(queries, key_rows, value_rows, key_limit, causal):
    blocked, starts = query_blocks(queries)
    key_heads = split_heads(key_rows)
    value_heads = split_heads(value_rows)

    def one_block(packed):
        query_part, start_row = packed
        scores = masked_scores(query_part, key_heads, start_row, key_limit, causal)
        row_peak = jnp.max(scores, -1, keepdims=True)
        exp_scores = jnp.exp(scores - row_peak)
        row_total = jnp.sum(exp_scores, -1, keepdims=True)
        prob_rows = (exp_scores / row_total).astype(jnp.bfloat16)
        attended = jnp.einsum(
            "hqk,khd->qhd", prob_rows, value_heads, preferred_element_type=jnp.float32
        )
        return (attended.astype(jnp.bfloat16), (row_peak + jnp.log(row_total))[..., 0])

    attended, log_total = lax.map(one_block, (blocked, starts))
    return (attended.reshape(queries.shape), log_total)


def attend_back(queries, key_rows, value_rows, grad_rows, log_total, key_limit, causal):
    blocked, starts = query_blocks(queries)
    grad_blocked, _ = query_blocks(grad_rows)
    key_heads = split_heads(key_rows)
    value_heads = split_heads(value_rows)
    score_scale = 1.0 / math.sqrt(HEAD_DIM)

    def one_block(running, packed):
        key_grad, value_grad = running
        query_part, grad_part, total_part, start_row = packed
        scores = masked_scores(query_part, key_heads, start_row, key_limit, causal)
        prob_rows = jnp.exp(scores - total_part[..., None])
        grad_probs = jnp.einsum(
            "qhd,khd->hqk", grad_part, value_heads, preferred_element_type=jnp.float32
        )
        inner = jnp.sum(prob_rows * grad_probs, -1, keepdims=True)
        grad_scores = (prob_rows * (grad_probs - inner) * score_scale).astype(jnp.bfloat16)
        query_grad = jnp.einsum(
            "hqk,khd->qhd", grad_scores, key_heads, preferred_element_type=jnp.float32
        )
        key_grad = key_grad + jnp.einsum(
            "hqk,qhd->khd", grad_scores, query_part, preferred_element_type=jnp.float32
        )
        value_grad = value_grad + jnp.einsum(
            "hqk,qhd->khd",
            prob_rows.astype(jnp.bfloat16),
            grad_part,
            preferred_element_type=jnp.float32,
        )
        return ((key_grad, value_grad), query_grad)

    empty_heads = jnp.zeros(key_heads.shape, jnp.float32)
    (key_grad, value_grad), query_grad = lax.scan(
        one_block, (empty_heads, empty_heads), (blocked, grad_blocked, log_total, starts)
    )
    return (
        query_grad.reshape(queries.shape),
        key_grad.reshape(key_rows.shape),
        value_grad.reshape(value_rows.shape),
    )


def self_back(
    source, packed, attended, log_total, first_grad, key_limit, causal, packed_weight, out_weight
):
    model_width = source.shape[1]
    branch_grad = first_grad.astype(jnp.bfloat16)
    out_grad = product_tn(attended, branch_grad)
    attended_grad = product_nt(branch_grad, out_weight).astype(jnp.bfloat16)
    query_grad, key_grad, value_grad = attend_back(
        packed[:, :model_width],
        packed[:, model_width : 2 * model_width],
        packed[:, 2 * model_width :],
        attended_grad,
        log_total,
        key_limit,
        causal,
    )
    packed_grad = jnp.concatenate([query_grad, key_grad, value_grad], 1).astype(jnp.bfloat16)
    return (product_nt(packed_grad, packed_weight), product_tn(source, packed_grad), out_grad)


def ffn_forward(hidden, in_weight, down_weight):
    hidden_low = hidden.astype(jnp.bfloat16)
    raised = product(hidden_low, in_weight)
    active = jax.nn.gelu(raised, approximate=False).astype(jnp.bfloat16)
    return (product(active, down_weight), (hidden_low, raised, active))


def ffn_backward(grad_rows, stored, in_weight, down_weight):
    hidden_low, raised, active = stored
    down_in = grad_rows.astype(jnp.bfloat16)
    raised_grad = (product_nt(down_in, down_weight) * gate_slope(raised)).astype(jnp.bfloat16)
    return (
        product_nt(raised_grad, in_weight),
        product_tn(hidden_low, raised_grad),
        product_tn(active, down_in),
    )


def encoder_forward(source, key_limit, weights):
    packed_weight, out_weight, cross_weight, in_weight, down_weight, gains, biases = weights
    model_width = source.shape[1]
    source_wide = source.astype(jnp.float32)
    packed = product(source, packed_weight).astype(jnp.bfloat16)
    attended, log_total = attend(
        packed[:, :model_width],
        packed[:, model_width : 2 * model_width],
        packed[:, 2 * model_width :],
        key_limit,
        False,
    )
    hidden, stored_one = norm_forward(
        source_wide + product(attended, out_weight), gains[0], biases[0]
    )
    branch, stored_ffn = ffn_forward(hidden, in_weight, down_weight)
    result, stored_two = norm_forward(hidden + branch + source_wide, gains[1], biases[1])
    result_low = result.astype(jnp.bfloat16)
    memory = product(result_low, cross_weight).astype(jnp.bfloat16)
    return (
        memory,
        result,
        (packed, attended, log_total, stored_one, stored_ffn, stored_two, result_low),
    )


def encoder_front(source, key_limit, weights, memory_grad):
    packed_weight, out_weight, cross_weight, in_weight, down_weight, gains, biases = weights
    _, _, kept = encoder_forward(source, key_limit, weights)
    packed, attended, log_total, stored_one, stored_ffn, stored_two, result_low = kept
    cross_grad = product_tn(result_low, memory_grad)
    last_grad, gain_two, bias_two = norm_backward(
        product_nt(memory_grad, cross_weight), stored_two, gains[1]
    )
    hidden_extra, in_grad, down_grad = ffn_backward(last_grad, stored_ffn, in_weight, down_weight)
    first_grad, gain_one, bias_one = norm_backward(last_grad + hidden_extra, stored_one, gains[0])
    kept_back = (packed, attended, log_total, first_grad, last_grad + first_grad)
    front = (
        cross_grad,
        in_grad,
        down_grad,
        jnp.stack([gain_one, gain_two]),
        jnp.stack([bias_one, bias_two]),
    )
    return (kept_back, front)


def encoder_rear(source, key_limit, weights, kept_back):
    packed, attended, log_total, first_grad, residual = kept_back
    source_extra, packed_grad, out_grad = self_back(
        source, packed, attended, log_total, first_grad, key_limit, False, weights[0], weights[1]
    )
    return (residual + source_extra, packed_grad, out_grad)


def encoder_backward(source, key_limit, weights, memory_grad):
    kept_back, front = encoder_front(source, key_limit, weights, memory_grad)
    source_grad, packed_grad, out_grad = encoder_rear(source, key_limit, weights, kept_back)
    return (source_grad, (packed_grad, out_grad) + front)


def decoder_step(target, target_limit, memory, source_limit, seed_rows, weights, cross_norm):
    packed_weight, out_weight, cross_weight, in_weight, down_weight, gains, biases = weights
    model_width = target.shape[1]
    target_wide = target.astype(jnp.float32)
    packed = product(target, packed_weight).astype(jnp.bfloat16)
    attended, log_self = attend(
        packed[:, :model_width],
        packed[:, model_width : 2 * model_width],
        packed[:, 2 * model_width :],
        target_limit,
        True,
    )
    hidden, stored_one = norm_forward(
        target_wide + product(attended, out_weight), gains[0], biases[0]
    )
    hidden_low = hidden.astype(jnp.bfloat16)
    asked = product(hidden_low, cross_weight[:, :model_width]).astype(jnp.bfloat16)
    context, log_cross = attend(
        asked, memory[:, :model_width], memory[:, model_width:], source_limit, False
    )
    mixed, stored_mid = norm_forward(
        hidden + product(context, cross_weight[:, model_width:]), cross_norm[0], cross_norm[1]
    )
    branch, stored_ffn = ffn_forward(mixed, in_weight, down_weight)
    result, stored_two = norm_forward(mixed + branch + target_wide, gains[1], biases[1])
    last_grad, gain_two, bias_two = norm_backward(
        seed_rows.astype(jnp.float32), stored_two, gains[1]
    )
    mixed_extra, in_grad, down_grad = ffn_backward(last_grad, stored_ffn, in_weight, down_weight)
    middle_grad, cross_gain, cross_bias = norm_backward(
        last_grad + mixed_extra, stored_mid, cross_norm[0]
    )
    branch_grad = middle_grad.astype(jnp.bfloat16)
    exit_grad = product_tn(context, branch_grad)
    context_grad = product_nt(branch_grad, cross_weight[:, model_width:]).astype(jnp.bfloat16)
    asked_grad, key_grad, value_grad = attend_back(
        asked,
        memory[:, :model_width],
        memory[:, model_width:],
        context_grad,
        log_cross,
        source_limit,
        False,
    )
    asked_low = asked_grad.astype(jnp.bfloat16)
    memory_grad = jnp.concatenate([key_grad, value_grad], 1).astype(jnp.bfloat16)
    entry_grad = product_tn(hidden_low, asked_low)
    first_grad, gain_one, bias_one = norm_backward(
        middle_grad + product_nt(asked_low, cross_weight[:, :model_width]), stored_one, gains[0]
    )
    target_extra, packed_grad, out_grad = self_back(
        target,
        packed,
        attended,
        log_self,
        first_grad,
        target_limit,
        True,
        packed_weight,
        out_weight,
    )
    target_grad = last_grad + first_grad + target_extra
    grads = (
        packed_grad,
        out_grad,
        jnp.concatenate([entry_grad, exit_grad], 1),
        in_grad,
        down_grad,
        jnp.stack([gain_one, gain_two]),
        jnp.stack([bias_one, bias_two]),
    )
    return (result, target_grad, memory_grad, grads, jnp.stack([cross_gain, cross_bias]))


def local(
    inputs,
    lengths,
    cotangent,
    qkv_weight,
    out_weight,
    cross_weight,
    ffn_in,
    ffn_out,
    norm_gain,
    norm_bias,
    cross_norm,
):
    weights = (
        qkv_weight[0],
        out_weight[0],
        cross_weight[0],
        ffn_in[0],
        ffn_out[0],
        norm_gain[0],
        norm_bias[0],
    )
    own_rows = inputs[0]
    own_limits = lengths[0]
    micro_count = own_rows.shape[0]
    seq_len = own_rows.shape[1]
    model_width = own_rows.shape[2]
    first_section = lax.axis_index("section") == 0
    norm_empty = jnp.zeros((2, model_width), jnp.float32)
    grads_empty = jax.tree.map(zeros_wide, weights)

    def encode_all():

        def encode_one(packed):
            memory, result, _ = encoder_forward(packed[0], packed[1], weights)
            return (memory, result)

        return lax.map(encode_one, (own_rows, own_limits))

    def forward_spare():
        return (
            jnp.zeros((micro_count, seq_len, 2 * model_width), jnp.bfloat16),
            jnp.zeros(own_rows.shape, jnp.float32),
        )

    memory_all, encoded = lax.cond(first_section, encode_all, forward_spare)
    memory_in, limits_in = passed_along((memory_all, own_limits), "section", 1)

    def decode_all():

        def decode_one(running, packed):
            target, target_limit, memory, source_limit, seed_rows = packed
            result, target_grad, memory_grad, grads, norm_grad = decoder_step(
                target, target_limit, memory, source_limit, seed_rows, weights, cross_norm
            )
            return (
                (tree_add(running[0], grads), running[1] + norm_grad),
                (result, target_grad, memory_grad),
            )

        running, outputs = lax.scan(
            decode_one,
            (grads_empty, norm_empty),
            (own_rows, own_limits, memory_in, limits_in, cotangent),
        )
        return (outputs, running)

    def decode_spare():
        empty_rows = jnp.zeros(own_rows.shape, jnp.float32)
        return (
            (empty_rows, empty_rows, jnp.zeros(memory_all.shape, jnp.bfloat16)),
            (grads_empty, norm_empty),
        )

    (decoded, target_part, memory_grads), (decoder_grads, norm_sum) = lax.cond(
        first_section, decode_spare, decode_all
    )
    memory_back = passed_along(memory_grads, "section", -1)

    def encode_back():

        def back_one(running, packed):
            source_grad, grads = encoder_backward(packed[0], packed[1], weights, packed[2])
            return (tree_add(running, grads), source_grad)

        running, source_grads = lax.scan(back_one, grads_empty, (own_rows, own_limits, memory_back))
        return (source_grads, running)

    def back_spare():
        return (jnp.zeros((micro_count, seq_len, model_width), jnp.float32), grads_empty)

    source_part, encoder_grads = lax.cond(first_section, encode_back, back_spare)
    layer_rows = jnp.where(first_section, encoded, decoded)
    section_grads = tree_pick(first_section, encoder_grads, decoder_grads)
    norm_in = passed_along(norm_sum, "section", -1)
    norm_row = jnp.where(first_section, norm_in[0], norm_sum[1])
    summed = lax.psum(
        (
            section_grads[0],
            section_grads[1],
            section_grads[2],
            section_grads[3],
            section_grads[4],
            section_grads[5],
            section_grads[6],
            norm_row,
        ),
        "dp",
    )
    input_rows = jnp.where(first_section, source_part, target_part)
    return (
        layer_rows[None],
        input_rows[None],
        summed[0][None],
        summed[1][None],
        summed[2][None],
        summed[3][None],
        summed[4][None],
        summed[5][None],
        summed[6][None],
        summed[7][None],
    )


def solution(mesh):
    in_specs = (
        P("section", "dp", None, None),
        P("section", "dp"),
        P("dp", None, None),
        P("section", None, None),
        P("section", None, None),
        P("section", None, None),
        P("section", None, None),
        P("section", None, None),
        P("section", None, None),
        P("section", None, None),
        P(),
    )
    out_specs = (
        P("section", "dp", None, None),
        P("section", "dp", None, None),
        P("section", None, None),
        P("section", None, None),
        P("section", None, None),
        P("section", None, None),
        P("section", None, None),
        P("section", None, None),
        P("section", None, None),
        P("section", None),
    )
    return jax.shard_map(local, mesh=mesh, in_specs=in_specs, out_specs=out_specs, check_vma=False)
```

profile of v0, /device:TPU:0, one launch (start us, length us, event | category | flops | bytes accessed | tf_op | source)
XLA Modules:
  0.0 2240.8 jit_solution(8219689581561794838)
XLA Ops:
  7.2 262.4 %conditional.3 = (bf16[2,1024,1024]{2,1,0:T(8,128)(2,1)}, f32[2,1024,512]{2,1,0:T(8,128)}) conditional(s32[]{:T(128)} %convert_element_type.162, () %tuple.72, (bf16[2,1024,512]{2,1,0:T(8,128)(2,1)}, bf16[512,1536]{1,0:T(8,128)(2,1)}, s32[2]{0:T(128)}, bf16[512,512]{1,0:T(8,128)(2,1)}, f32[2,512]{1,0:T(2,128)}, /*index=5*/f32[2,512]{1,0:T(2,128)}, ...), branch_computations={%region_0.0_spmd, %region_1.12_spmd} | conditional | flops 8778944512 | bytes 173194048 | solution.py:376
  7.3 260.6 %while.171 = (s32[]{:T(128)}, bf16[2,1024,1024]{2,1,0:T(8,128)(2,1)}, f32[2,1024,512]{2,1,0:T(8,128)}, bf16[2,1024,512]{2,1,0:T(8,128)(2,1)}, bf16[512,1536]{1,0...) while((s32[]{:T(128)}, ...), condition=%wide.region_11.11_spmd, body=%wide.region_2.10_spmd.sunk | while | flops 8778944512 | bytes 173193904 | solution.py:368
  23.2 74.3 %while.178 = (s32[]{:T(128)}, bf16[2,512,8,64]{1,3,2,0:T(8,128)(2,1)}, s32[]{:T(128)}, bf16[2,512,8,64]{1,3,2,0:T(8,128)(2,1)S(1)}, bf16[1024,8,64]{0,2,1:T(8,12...) while((s32[]{:T(128)}, bf16[2,512,8,64]{1,3,2,0:T(8,128)(2,1)}, s32[]{:T(128)}, ...), condition=%wide.region_6.5_spmd, body=%wide.region_3.4_spmd.sunk | while | flops 1107560448 | bytes 74483840 | solution.py:112
  23.7 8.2 fusion.708
  31.9 19.0 fusion.709
  50.9 9.3 fusion.710
  60.8 8.2 fusion.708
  68.9 19.0 fusion.709
  88.0 9.3 fusion.710
  102.3 25.6 %fusion.703 = (f32[1024]{0:T(1024)S(1)}, f32[1024,512]{0,1:T(8,128)S(1)}) fusion(bf16[1,1024,512]{1,2,0:T(8,128)(2,1)S(1)} %copy-done.53, bf16[2048,512]{1,0:T(8,128)(2,1)} %get-tuple-element.2630, bf16[512,2048]{1,0:T(8,128)(2,1)} %get-tuple-element.2629, f32[1024,512]{0,1:T(8,128)} %copy-done.41, f32[512]{0:T(512)S(1)} %bitcast.789, ...), kind=kOutput, calls=%fused_computation.466.clone.1 | convolution fusion | flops 4438096896 | bytes 9453568 | tf_op jit(solution)/shard_map/cond/branch_1_fun/while/body/eval_jaxpr/dot_general | solution.py:19
  153.0 74.5 %while.178 = (s32[]{:T(128)}, bf16[2,512,8,64]{1,3,2,0:T(8,128)(2,1)}, s32[]{:T(128)}, bf16[2,512,8,64]{1,3,2,0:T(8,128)(2,1)S(1)}, bf16[1024,8,64]{0,2,1:T(8,12...) while((s32[]{:T(128)}, bf16[2,512,8,64]{1,3,2,0:T(8,128)(2,1)}, s32[]{:T(128)}, ...), condition=%wide.region_6.5_spmd, body=%wide.region_3.4_spmd.sunk | while | flops 1107560448 | bytes 74483840 | solution.py:112
  153.6 8.2 fusion.708
  161.7 19.0 fusion.709
  180.8 9.3 fusion.710
  190.6 8.2 fusion.708
  198.8 19.0 fusion.709
  217.8 9.3 fusion.710
  232.4 25.4 %fusion.703 = (f32[1024]{0:T(1024)S(1)}, f32[1024,512]{0,1:T(8,128)S(1)}) fusion(bf16[1,1024,512]{1,2,0:T(8,128)(2,1)S(1)} %copy-done.53, bf16[2048,512]{1,0:T(8,128)(2,1)} %get-tuple-element.2630, bf16[512,2048]{1,0:T(8,128)(2,1)} %get-tuple-element.2629, f32[1024,512]{0,1:T(8,128)} %copy-done.41, f32[512]{0:T(512)S(1)} %bitcast.789, ...), kind=kOutput, calls=%fused_computation.466.clone.1 | convolution fusion | flops 4438096896 | bytes 9453568 | tf_op jit(solution)/shard_map/cond/branch_1_fun/while/body/eval_jaxpr/dot_general | solution.py:19
  269.6 6.2 copy.93
  278.7 5.2 collective-permute-done.1
  286.5 22.9 %conditional.4 = (f32[2,1024,512]{1,2,0:T(8,128)}, f32[2,1024,512]{1,2,0:T(8,128)}, bf16[2,1024,1024]{1,2,0:T(8,128)(2,1)}, f32[512,1536]{1,0:T(8,128)}, f32[512...) conditional(s32[]{:T(128)} %convert_element_type.162, ...), branch_computations={%region_12.47_spmd, %region_47.48_spmd} | conditional | flops 30551339008 | bytes 1373121664 | solution.py:405
  309.4 6.3 copy.98
  318.9 942.4 %collective-permute-done.2 = bf16[2,1024,1024]{2,1,0:T(8,128)(2,1)} collective-permute-done((bf16[2,1024,1024]{2,1,0:T(8,128)(2,1)}, bf16[2,1024,1024]{2,1,0:T(8,128)(2,1)}, u32[]{:S(2)}, u32[]{:S(2)}) %collective-permute-start.2) | collective-permute-done | bytes 4194336 | tf_op jit(solution)/shard_map/ppermute | solution.py:15
  1261.2 522.7 %conditional.5 = (f32[2,1024,512]{2,1,0:T(8,128)}, f32[512,1536]{1,0:T(8,128)}, f32[512,512]{1,0:T(8,128)}, f32[512,1024]{1,0:T(8,128)}, f32[512,2048]{1,0:T(8,1...) conditional(s32[]{:T(128)} %convert_element_type.162, () %tuple.76, ...), branch_computations={%region_48.49_spmd, %region_49.71_spmd} | conditional | flops 25568229376 | bytes 631725504 | solution.py:422
  1261.2 517.2 %while.168 = (s32[]{:T(128)}, f32[512,1536]{1,0:T(8,128)}, f32[512,512]{1,0:T(8,128)}, f32[512,1024]{1,0:T(8,128)}, f32[512,2048]{1,0:T(8,128)}, /*index=5*/f32[...) while((s32[]{:T(128)}, f32[512,1536]{1,0:T(8,128)}, ...), condition=%wide.region_70.70_spmd.clone, body=%wide.region_50.69_spmd.clone.sunk | while | flops 25568229376 | bytes 631725248 | solution.py:416
  1276.1 25.9 %while.172 = (s32[]{:T(128)}, bf16[2,512,8,64]{1,3,2,0:T(8,128)(2,1)}, f32[2,8,512]{2,1,0:T(8,128)S(1)}, s32[]{:T(128)}, bf16[2,512,8,64]{1,3,2,0:T(8,128)(2,1)S...) while((s32[]{:T(128)}, bf16[2,512,8,64]{1,3,2,0:T(8,128)(2,1)}, ...), condition=%wide.region_55.54_spmd, body=%wide.region_52.53_spmd.sunk | while | flops 1124332544 | bytes 62001316 | solution.py:112
  1306.8 19.3 fusion.590
  1338.9 4.9 fusion.592
  1351.5 4.7 select_add_fusion.11
  1368.6 132.6 %while.173 = (s32[]{:T(128)}, f32[1024,8,64]{0,2,1:T(8,128)}, f32[1024,8,64]{0,2,1:T(8,128)S(1)}, bf16[2,512,8,64]{1,3,2,0:T(8,128)(2,1)}, bf16[2,512,8,64]{1,3,...) while((s32[]{:T(128)}, f32[1024,8,64]{0,2,1:T(8,128)}, ...), condition=%wide.region_65.64_spmd.clone, body=%wide.region_63.63_spmd.clone.sunk | while | flops 2745183232 | bytes 270584032 | solution.py:148
  1369.3 5.3 subtract_exponential_fusion.10
  1380.5 8.1 fusion.608
  1388.6 22.7 %fusion.609 = bf16[2,512,8,64]{1,3,2,0:T(8,128)(2,1)} fusion(bf16[2,512,8,64]{1,3,2,0:T(8,128)(2,1)} %get-tuple-element.2905, s32[]{:T(128)S(6)} %copy.317, bf16[1024,8,64]{0,2,1:T(8,128)(2,1)} %get-tuple-element.2920, f32[8,512,1024]{2,1,0:T(8,128)} %copy-done.2, f32[8,512,1024]{2,1,0:T(8,128)} %fusion.608), kind=kOutput, calls=%fused_computation.343.clone.1 | convolution fusion | flops 557847552 | bytes 69206016 | tf_op jit(solution)/shard_map/cond/branch_1_fun/while/body/eval_jaxpr/while/body/eval_jaxpr/hqk,khd->qhd/dot_general | solution.py:133
  1411.3 23.3 %bitcast_add_fusion.12 = f32[1024,8,64]{0,2,1:T(8,128)} fusion(f32[1024,8,64]{0,2,1:T(8,128)} %get-tuple-element.2903, f32[8,512,1024]{2,1,0:T(8,128)} %copy-done.2, f32[8,512,1024]{2,1,0:T(8,128)} %fusion.608, pred[]{:T(512)S(6)} %compare.16, bf16[2,512,8,64]{1,3,2,0:T(8,128)(2,1)} %get-tuple-element.2918, s32[]{:T(128)S(6)} %copy.317), kind=kOutput, calls=%fused_computation.341.clone.1 | convolution fusion | flops 558896128 | bytes 71827464 | tf_op jit(solution)/shard_map/cond/branch_1_fun/while/body/eval_jaxpr/while/body/eval_jaxpr/hqk,qhd->khd/dot_general | solution.py:136
  1435.2 5.3 subtract_exponential_fusion.10
  1446.4 8.1 fusion.608
  1454.5 22.7 %fusion.609 = bf16[2,512,8,64]{1,3,2,0:T(8,128)(2,1)} fusion(bf16[2,512,8,64]{1,3,2,0:T(8,128)(2,1)} %get-tuple-element.2905, s32[]{:T(128)S(6)} %copy.317, bf16[1024,8,64]{0,2,1:T(8,128)(2,1)} %get-tuple-element.2920, f32[8,512,1024]{2,1,0:T(8,128)} %copy-done.2, f32[8,512,1024]{2,1,0:T(8,128)} %fusion.608), kind=kOutput, calls=%fused_computation.343.clone.1 | convolution fusion | flops 557847552 | bytes 69206016 | tf_op jit(solution)/shard_map/cond/branch_1_fun/while/body/eval_jaxpr/while/body/eval_jaxpr/hqk,khd->qhd/dot_general | solution.py:133
  1477.2 23.9 %bitcast_add_fusion.12 = f32[1024,8,64]{0,2,1:T(8,128)} fusion(f32[1024,8,64]{0,2,1:T(8,128)} %get-tuple-element.2903, f32[8,512,1024]{2,1,0:T(8,128)} %copy-done.2, f32[8,512,1024]{2,1,0:T(8,128)} %fusion.608, pred[]{:T(512)S(6)} %compare.16, bf16[2,512,8,64]{1,3,2,0:T(8,128)(2,1)} %get-tuple-element.2918, s32[]{:T(128)S(6)} %copy.317), kind=kOutput, calls=%fused_computation.341.clone.1 | convolution fusion | flops 558896128 | bytes 71827464 | tf_op jit(solution)/shard_map/cond/branch_1_fun/while/body/eval_jaxpr/while/body/eval_jaxpr/hqk,qhd->khd/dot_general | solution.py:136
  1509.3 5.6 convolution_add_fusion.11
  1529.8 25.8 %while.172 = (s32[]{:T(128)}, bf16[2,512,8,64]{1,3,2,0:T(8,128)(2,1)}, f32[2,8,512]{2,1,0:T(8,128)S(1)}, s32[]{:T(128)}, bf16[2,512,8,64]{1,3,2,0:T(8,128)(2,1)S...) while((s32[]{:T(128)}, bf16[2,512,8,64]{1,3,2,0:T(8,128)(2,1)}, ...), condition=%wide.region_55.54_spmd, body=%wide.region_52.53_spmd.sunk | while | flops 1124332544 | bytes 62001316 | solution.py:112
  1536.9 4.7 fusion.597
  1549.6 4.7 fusion.597
  1560.4 19.3 fusion.590
  1583.4 5.1 select_add_fusion.10
  1593.2 4.9 fusion.592
  1598.0 6.7 select_add_fusion.12
  1607.9 6.9 select_add_fusion.11
  1629.8 132.6 %while.173 = (s32[]{:T(128)}, f32[1024,8,64]{0,2,1:T(8,128)}, f32[1024,8,64]{0,2,1:T(8,128)S(1)}, bf16[2,512,8,64]{1,3,2,0:T(8,128)(2,1)}, bf16[2,512,8,64]{1,3,...) while((s32[]{:T(128)}, f32[1024,8,64]{0,2,1:T(8,128)}, ...), condition=%wide.region_65.64_spmd.clone, body=%wide.region_63.63_spmd.clone.sunk | while | flops 2745183232 | bytes 270584032 | solution.py:148
  1630.6 5.3 subtract_exponential_fusion.10
  1641.7 8.1 fusion.608
  1649.9 22.7 %fusion.609 = bf16[2,512,8,64]{1,3,2,0:T(8,128)(2,1)} fusion(bf16[2,512,8,64]{1,3,2,0:T(8,128)(2,1)} %get-tuple-element.2905, s32[]{:T(128)S(6)} %copy.317, bf16[1024,8,64]{0,2,1:T(8,128)(2,1)} %get-tuple-element.2920, f32[8,512,1024]{2,1,0:T(8,128)} %copy-done.2, f32[8,512,1024]{2,1,0:T(8,128)} %fusion.608), kind=kOutput, calls=%fused_computation.343.clone.1 | convolution fusion | flops 557847552 | bytes 69206016 | tf_op jit(solution)/shard_map/cond/branch_1_fun/while/body/eval_jaxpr/while/body/eval_jaxpr/hqk,khd->qhd/dot_general | solution.py:133
  1672.5 23.3 %bitcast_add_fusion.12 = f32[1024,8,64]{0,2,1:T(8,128)} fusion(f32[1024,8,64]{0,2,1:T(8,128)} %get-tuple-element.2903, f32[8,512,1024]{2,1,0:T(8,128)} %copy-done.2, f32[8,512,1024]{2,1,0:T(8,128)} %fusion.608, pred[]{:T(512)S(6)} %compare.16, bf16[2,512,8,64]{1,3,2,0:T(8,128)(2,1)} %get-tuple-element.2918, s32[]{:T(128)S(6)} %copy.317), kind=kOutput, calls=%fused_computation.341.clone.1 | convolution fusion | flops 558896128 | bytes 71827464 | tf_op jit(solution)/shard_map/cond/branch_1_fun/while/body/eval_jaxpr/while/body/eval_jaxpr/hqk,qhd->khd/dot_general | solution.py:136
  1696.5 5.3 subtract_exponential_fusion.10
  1707.6 8.1 fusion.608
  1715.8 22.7 %fusion.609 = bf16[2,512,8,64]{1,3,2,0:T(8,128)(2,1)} fusion(bf16[2,512,8,64]{1,3,2,0:T(8,128)(2,1)} %get-tuple-element.2905, s32[]{:T(128)S(6)} %copy.317, bf16[1024,8,64]{0,2,1:T(8,128)(2,1)} %get-tuple-element.2920, f32[8,512,1024]{2,1,0:T(8,128)} %copy-done.2, f32[8,512,1024]{2,1,0:T(8,128)} %fusion.608), kind=kOutput, calls=%fused_computation.343.clone.1 | convolution fusion | flops 557847552 | bytes 69206016 | tf_op jit(solution)/shard_map/cond/branch_1_fun/while/body/eval_jaxpr/while/body/eval_jaxpr/hqk,khd->qhd/dot_general | solution.py:133
  1738.4 23.9 %bitcast_add_fusion.12 = f32[1024,8,64]{0,2,1:T(8,128)} fusion(f32[1024,8,64]{0,2,1:T(8,128)} %get-tuple-element.2903, f32[8,512,1024]{2,1,0:T(8,128)} %copy-done.2, f32[8,512,1024]{2,1,0:T(8,128)} %fusion.608, pred[]{:T(512)S(6)} %compare.16, bf16[2,512,8,64]{1,3,2,0:T(8,128)(2,1)} %get-tuple-element.2918, s32[]{:T(128)S(6)} %copy.317), kind=kOutput, calls=%fused_computation.341.clone.1 | convolution fusion | flops 558896128 | bytes 71827464 | tf_op jit(solution)/shard_map/cond/branch_1_fun/while/body/eval_jaxpr/while/body/eval_jaxpr/hqk,qhd->khd/dot_general | solution.py:136
  1770.6 7.0 convolution_add_fusion.11
  1784.0 5.4 select_bitcast_fusion
  1789.3 5.1 select_bitcast_fusion.1
  1806.4 5.4 copy.97
  1811.8 5.7 copy.99
  1818.2 83.0 %all-reduce = (f32[1,2,512]{2,1,0:T(2,128)}, f32[1,2,512]{2,1,0:T(2,128)}, f32[1,512]{1,0:T(1,128)}) all-reduce(f32[1,2,512]{2,1,0:T(2,128)S(1)} %get-tuple-element.1551, f32[1,2,512]{2,1,0:T(2,128)S(1)} %get-tuple-element.1550, f32[1,512]{1,0:T(1,128)S(1)} %broadcast_select_fusion), channel_id=1, replica_groups=mesh['section'=2,'dp'=16] {'dp'}, use_global_device_ids=true, to_apply=%region_76.77 | all-reduce | flops 2560 | bytes 20480 | tf_op jit(solution)/shard_map/psum | solution.py:427
  1901.3 9.3 select_bitcast_fusion.2
  1910.5 310.1 %all-reduce.4.cloned.1.call-done = (f32[1,512,1536]{2,1,0:T(8,128)}, f32[1,512,512]{2,1,0:T(8,128)}, f32[1,512,1024]{2,1,0:T(8,128)}, f32[1,512,2048]{2,1,0:T(8,128)}, f32[1,2048,512]{2,1,0:T(8,128)}) async-done(((f32[1,512,1536]{2,1,0:T(8,128)}, f32[1,512,512]{2,1,0:T(8,128)}, f32[1,512,1024]{2,1,0:T(8,128)}, f32[1,512,2048]{2,1,0:T(8,128)}, f32[1,2048,512]{2,1,0:T(8,128)}), (f32[1,512,1536]{2,1,0:T(8,128)}, ...) | async-done | bytes 14680080 | tf_op jit(solution)/shard_map/psum | solution.py:427
  (392 shorter events, 295.2 us)
Async XLA Ops:
  7.2 2213.5 %all-reduce.4.cloned.1.call-start = ((), (), s32[]{:S(2)}) async-start(), calls=%async_computation | async-start | bytes 29360128 | tf_op jit(solution)/shard_map/psum | solution.py:427
  7.5 5.3 copy-start.141
  31.9 19.1 copy-start.72
  68.9 19.1 copy-start.72
  102.3 26.0 %copy-start.114 = (f32[1,512]{1,0:T(1,128)S(1)}, f32[1,512]{1,0:T(1,128)}, u32[]{:S(2)}) copy-start(f32[1,512]{1,0:T(1,128)} %get-tuple-element.2558) | copy-start | bytes 6148 | tf_op jit(solution)/shard_map/cond/branch_1_fun/while
  102.3 26.0 %copy-start.115 = (f32[1,512]{1,0:T(1,128)S(1)}, f32[1,512]{1,0:T(1,128)}, u32[]{:S(2)}) copy-start(f32[1,512]{1,0:T(1,128)} %get-tuple-element.2557) | copy-start | bytes 6148 | tf_op jit(solution)/shard_map/cond/branch_1_fun/while
  128.3 4.6 copy-start.65
  137.3 5.3 copy-start.141
  161.7 19.1 copy-start.72
  198.8 19.1 copy-start.72
  232.4 25.8 %copy-start.114 = (f32[1,512]{1,0:T(1,128)S(1)}, f32[1,512]{1,0:T(1,128)}, u32[]{:S(2)}) copy-start(f32[1,512]{1,0:T(1,128)} %get-tuple-element.2558) | copy-start | bytes 6148 | tf_op jit(solution)/shard_map/cond/branch_1_fun/while
  232.4 25.8 %copy-start.115 = (f32[1,512]{1,0:T(1,128)S(1)}, f32[1,512]{1,0:T(1,128)}, u32[]{:S(2)}) copy-start(f32[1,512]{1,0:T(1,128)} %get-tuple-element.2557) | copy-start | bytes 6148 | tf_op jit(solution)/shard_map/cond/branch_1_fun/while
  258.2 4.6 copy-start.65
  269.6 7.8 copy-start.144
  275.8 8.3 collective-permute-start
  277.4 6.5 collective-permute-start.1
  309.4 7.6 copy-start.56
  315.7 945.5 %collective-permute-start.2 = (bf16[2,1024,1024]{2,1,0:T(8,128)(2,1)}, bf16[2,1024,1024]{2,1,0:T(8,128)(2,1)}, u32[]{:S(2)}, u32[]{:S(2)}) collective-permute-start(bf16[2,1024,1024]{2,1,0:T(8,128)(2,1)} %copy.98), channel_id=1, source_target_pairs={{16,0},{17,1},{18,2},{19,3},{20,4},{21,5},{22,6},{23,7},{24,8},{25... | collective-permute-start | bytes 12582920 | tf_op jit(solution)/shard_map/ppermute | solution.py:15
  1279.2 4.0 copy-start.73
  1291.9 4.0 copy-start.73
  1302.0 4.3 copy-start.18
  1302.0 4.3 copy-start.33
  1302.0 3.4 copy-start.31
  1302.0 3.4 copy-start.42
  1306.8 19.3 copy-start.140
  1326.1 3.6 copy-start.97
  1326.1 3.6 copy-start.104
  1329.8 4.5 copy-start.69
  1338.9 9.4 copy-start.60
  1359.6 8.9 copy-start.10
  1369.3 5.4 copy-start.16
  1374.7 5.8 copy-start.2
  1435.2 5.4 copy-start.16
  1440.6 5.8 copy-start.2
  1506.3 3.1 copy-start.43
  1532.9 4.0 copy-start.73
  1545.6 4.0 copy-start.73
  1555.6 4.3 copy-start.18
  1555.6 4.3 copy-start.33
  1555.7 3.4 copy-start.31
  1555.7 3.4 copy-start.42
  1560.4 19.3 copy-start.140
  1579.7 3.6 copy-start.97
  1579.7 3.6 copy-start.104
  1583.4 5.1 copy-start.69
  1593.2 11.6 copy-start.60
  1617.2 3.7 copy-start.26
  1620.9 8.9 copy-start.10
  1630.5 5.4 copy-start.16
  1635.9 5.8 copy-start.2
  1696.5 5.4 copy-start.16
  1701.8 5.8 copy-start.2
  1767.5 3.1 copy-start.43
  1783.9 5.4 copy-start.88
  1789.3 5.1 copy-start.77
  1794.4 3.5 copy-start.64
  1794.4 5.9 copy-start.91
  1805.1 12.4 collective-permute-start.3
  1811.8 5.7 copy-start.123
  1811.8 5.7 copy-start.126
  2220.7 3.9 copy-start.105
  2220.7 4.9 copy-start.95
  2224.6 3.3 copy-start.79
  2227.9 3.7 copy-start.78
  (34 other events, 65.4 us)
Sparse Core Ops, SparseCore 0:
  1804.6 416.0 all-reduce.3
where the time goes:
time: 2240 us
  waiting for transfers between devices  1260 us (56%)
  matrix products  544 us (24%)
  local copies, waits for them, and re-layouts  177 us (8%)
  other arithmetic  142 us (6%)
  blocking collectives  83 us (4%)
    ppermute x4, waiting for transfers between devices, passed_along(): return lax.ppermute(block, axis, route)  948 us
    psum x1, waiting for transfers between devices, local(): lax.psum((section_grads[0], section_grads[1], section_grads[2], section_g...  310 us
    dot_general x16, matrix products, product(): return jnp.dot(left_side, right_side, preferred_element_type=jnp.float32)  115 us
    dot_general x4, matrix products, one_block(): jnp.einsum('hqk,qhd->khd', grad_scores, query_part, preferred_element_typ...  94.5 us
    dot_general x4, matrix products, one_block(): jnp.einsum('hqk,khd->qhd', grad_scores, key_heads, preferred_element_type...  90.7 us
    psum x1, blocking collectives, local(): lax.psum((section_grads[0], section_grads[1], section_grads[2], section_g...  83 us
    sub x4, other arithmetic, one_block(): exp_scores = jnp.exp(scores - row_peak)  76.2 us
    dot_general x12, matrix products, masked_scores(): jnp.einsum('qhd,khd->hqk', query_part, key_heads, preferred_element_type=...  64.1 us
  transfers between devices with their start and end apart: 5, of which 4 were waited for; matrix products, arithmetic and copies ran while one was open for 1% of the time, Pallas kernels for 0%

commit v1 on v0

v1 whole, which is shorter than its diff:
```python
from functools import partial
import math

import jax
import jax.numpy as jnp
from jax import lax
from jax.experimental import pallas as pl
from jax.experimental.pallas import tpu as pltpu
from jax.sharding import PartitionSpec as P

F32, BF16 = jnp.float32, jnp.bfloat16
HEAD_DIM = 64
PAIR = 2 * HEAD_DIM
LOG2E = math.log2(math.e)
NEG = -1e30
EPS = 1e-05
SCALE = 1.0 / math.sqrt(HEAD_DIM)
VMEM_LIMIT = 56 << 20


def nn(left, right):
    return lax.dot_general(left, right, (((1,), (0,)), ((), ())), preferred_element_type=F32)


def nt(left, right):
    return lax.dot_general(left, right, (((1,), (1,)), ((), ())), preferred_element_type=F32)


def tn(left, right):
    return lax.dot_general(left, right, (((0,), (0,)), ((), ())), preferred_element_type=F32)


def lanes(shape):
    return lax.broadcasted_iota(jnp.int32, shape, 1)


def rows_of(shape):
    return lax.broadcasted_iota(jnp.int32, shape, 0)


def norm_forward(field, gain, bias):
    centred = field - jnp.mean(field, -1, keepdims=True)
    inverse = lax.rsqrt(jnp.mean(centred * centred, -1, keepdims=True) + EPS)
    normed = centred * inverse
    return normed * gain + bias, normed, inverse


def norm_backward(grad, normed, inverse, gain):
    scaled = grad * gain
    inner = (
        scaled
        - jnp.mean(scaled, -1, keepdims=True)
        - normed * jnp.mean(scaled * normed, -1, keepdims=True)
    )
    gain_grad = jnp.sum(grad * normed, 0, keepdims=True)
    return inner * inverse, gain_grad, jnp.sum(grad, 0, keepdims=True)


def gelu_parts(raised):
    cumulative = 0.5 * (1.0 + lax.erf(raised * (1.0 / math.sqrt(2.0))))
    density = jnp.exp(-0.5 * raised * raised) * (1.0 / math.sqrt(2.0 * math.pi))
    return raised * cumulative, cumulative + raised * density


def split3(value):
    high = value.astype(BF16)
    rest = value - high.astype(F32)
    middle = rest.astype(BF16)
    return high, middle, (rest - middle.astype(F32)).astype(BF16)


def attend_body(limit, q_ref, k_ref, v_ref, o_ref, l_ref, ke, ve, causal, block):
    total = q_ref.shape[0]
    lane = lanes((total, PAIR))
    ke[:, :PAIR] = k_ref[...]
    ke[:, PAIR:] = jnp.where((lane == 3) & (rows_of((total, PAIR)) >= limit), NEG, 0.0).astype(BF16)
    ve[:, :PAIR] = v_ref[...]
    ve[:, PAIR:] = jnp.ones((total, PAIR), BF16)
    lane_q = lanes((block, PAIR))
    first = lane_q < HEAD_DIM
    aux = jnp.where(lane_q == 3, 1.0, 0.0).astype(BF16)
    for j in range(total // block):
        here = pl.ds(j * block, block)
        seen = (j + 1) * block if causal else total
        q_pair = q_ref[here, :]
        zero = jnp.zeros_like(q_pair)
        parts = []
        for h in range(2):
            own = first if h == 0 else jnp.logical_not(first)
            q_ext = jnp.concatenate([jnp.where(own, q_pair, zero), aux], 1)
            scores = nt(q_ext, ke[:seen, :])
            if causal:
                keep = lanes((block, block)) <= rows_of((block, block))
                edge = jnp.where(keep, scores[:, j * block :], NEG)
                scores = jnp.concatenate([scores[:, : j * block], edge], 1) if j else edge
            peak = jnp.max(scores, -1, keepdims=True)
            probs = jnp.exp2(scores - peak).astype(BF16)
            mixed = nn(probs, ve[:seen, :])
            sums = mixed[:, PAIR:]
            parts.append((mixed[:, :PAIR] / sums, peak + jnp.log2(sums)))
        o_ref[here, :] = jnp.where(first, parts[0][0], parts[1][0]).astype(BF16)
        l_ref[here, :] = jnp.where(first, parts[0][1], parts[1][1])


def attend_back_body(limit, q_ref, k_ref, v_ref, o_ref, l_ref, g_ref, scr, causal, block):
    ke, ve, dka, dva, dqa = scr
    total = q_ref.shape[0]
    lane = lanes((total, PAIR)) % HEAD_DIM
    ones = jnp.where(lane < 3, 1.0, 0.0)
    ke[:, :PAIR] = k_ref[...]
    outside = (lane == 3) & (rows_of((total, PAIR)) >= limit)
    ke[:, PAIR:] = jnp.where(outside, NEG, ones).astype(BF16)
    ve[:, :PAIR] = v_ref[...]
    ve[:, PAIR:] = ones.astype(BF16)
    lane_q = lanes((block, PAIR))
    first = lane_q < HEAD_DIM
    spot = lane_q % HEAD_DIM
    unit = jnp.where(spot == 3, 1.0, 0.0).astype(BF16)
    for j in range(total // block):
        here = pl.ds(j * block, block)
        low = j * block
        seen = low + block if causal else total
        q_pair = q_ref[here, :]
        g_pair = g_ref[here, :]
        zero = jnp.zeros_like(q_pair)
        product = g_pair.astype(F32) * o_ref[here, :].astype(F32)
        a, b, c = split3(-l_ref[here, :])
        aux_q = jnp.where(spot == 0, a, jnp.where(spot == 1, b, jnp.where(spot == 2, c, unit)))
        dqs = []
        for h in range(2):
            own = first if h == 0 else jnp.logical_not(first)
            inner = jnp.sum(jnp.where(own, product, 0.0), -1, keepdims=True)
            a, b, c = split3(jnp.broadcast_to(-inner, (block, PAIR)))
            aux_g = jnp.where(spot == 0, a, jnp.where(spot == 1, b, jnp.where(spot == 2, c, zero)))
            q_own = jnp.where(own, q_pair, zero)
            g_own = jnp.where(own, g_pair, zero)
            q_ext = jnp.concatenate([q_own, jnp.where(own, aux_q, zero)], 1)
            g_ext = jnp.concatenate([g_own, jnp.where(own, aux_g, zero)], 1)
            probs = jnp.exp2(nt(ke[:seen, :], q_ext))
            if causal:
                keep = rows_of((block, block)) <= lanes((block, block))
                edge = jnp.where(keep, probs[low:, :], 0.0)
                probs = jnp.concatenate([probs[:low, :], edge], 0) if j else edge
            slope = (probs * nt(ve[:seen, :], g_ext)).astype(BF16)
            dv = nn(probs.astype(BF16), g_own)
            dk = nn(slope, q_own)
            if h == 0 and causal:
                if j:
                    dva[:low, :] += dv[:low]
                    dka[:low, :] += dk[:low]
                dva[low:seen, :] = dv[low:]
                dka[low:seen, :] = dk[low:]
            elif h == 0 and j == 0:
                dva[...] = dv
                dka[...] = dk
            else:
                dva[:seen, :] += dv
                dka[:seen, :] += dk
            dqs.append(jnp.transpose(tn(k_ref[:seen, :], slope)))
        dqa[here, :] = (jnp.where(first, dqs[0], dqs[1]) * SCALE).astype(BF16)


def attend_scratch(total):
    return [
        pltpu.VMEM((total, 2 * PAIR), BF16),
        pltpu.VMEM((total, 2 * PAIR), BF16),
        pltpu.VMEM((total, PAIR), F32),
        pltpu.VMEM((total, PAIR), F32),
        pltpu.VMEM((total, PAIR), BF16),
    ]


def params(**extra):
    return pltpu.CompilerParams(vmem_limit_bytes=VMEM_LIMIT, **extra)


def smem():
    return pl.BlockSpec(memory_space=pltpu.SMEM)


def whole(array):
    zeros = (0,) * array.ndim
    return pl.BlockSpec(array.shape, lambda *_: zeros, pipeline_mode=pl.Buffered(1))


def column(total, shift=0):
    return pl.BlockSpec((total, PAIR), lambda p: (0, p + shift))


def self_forward(rows, weight, limit, causal):
    total, width = rows.shape
    pairs = width // PAIR
    block = min(256, total)

    def kernel(lim, x_ref, wq, wk, wv, q_ref, k_ref, v_ref, o_ref, l_ref, ke, ve):
        rows_in = x_ref[...]
        q_ref[...] = (nn(rows_in, wq[...]) * (SCALE * LOG2E)).astype(BF16)
        k_ref[...] = nn(rows_in, wk[...]).astype(BF16)
        v_ref[...] = nn(rows_in, wv[...]).astype(BF16)
        attend_body(lim[0], q_ref, k_ref, v_ref, o_ref, l_ref, ke, ve, causal, block)

    return pl.pallas_call(
        kernel,
        grid=(pairs,),
        in_specs=[smem(), whole(rows)] + [column(width, s * pairs) for s in range(3)],
        out_specs=[column(total)] * 5,
        out_shape=[jax.ShapeDtypeStruct((total, width), BF16)] * 4
        + [jax.ShapeDtypeStruct((total, width), F32)],
        scratch_shapes=attend_scratch(total)[:2],
        compiler_params=params(),
    )(limit, rows, weight, weight, weight)


def cross_forward(asked, memory, limit):
    total, width = asked.shape
    pairs = width // PAIR
    block = min(256, total)

    def kernel(lim, q_ref, k_ref, v_ref, o_ref, l_ref, ke, ve):
        attend_body(lim[0], q_ref, k_ref, v_ref, o_ref, l_ref, ke, ve, False, block)

    return pl.pallas_call(
        kernel,
        grid=(pairs,),
        in_specs=[smem(), column(total), column(total), column(total, pairs)],
        out_specs=[column(total)] * 2,
        out_shape=[
            jax.ShapeDtypeStruct((total, width), BF16),
            jax.ShapeDtypeStruct((total, width), F32),
        ],
        scratch_shapes=attend_scratch(total)[:2],
        compiler_params=params(),
    )(limit, asked, memory, memory)


def cross_backward(asked, memory, limit, context, logs, grad):
    total, width = asked.shape
    pairs = width // PAIR
    block = min(256, total)

    def kernel(lim, q_ref, k_ref, v_ref, o_ref, l_ref, g_ref, dq_ref, dk_ref, dv_ref, *scr):
        attend_back_body(lim[0], q_ref, k_ref, v_ref, o_ref, l_ref, g_ref, scr, False, block)
        dq_ref[...] = scr[4][...]
        dk_ref[...] = (scr[2][...] * (1.0 / LOG2E)).astype(BF16)
        dv_ref[...] = scr[3][...].astype(BF16)

    return pl.pallas_call(
        kernel,
        grid=(pairs,),
        in_specs=[smem(), column(total), column(total), column(total, pairs)] + [column(total)] * 3,
        out_specs=[column(total)] * 3,
        out_shape=[jax.ShapeDtypeStruct((total, width), BF16)] * 3,
        scratch_shapes=attend_scratch(total),
        compiler_params=params(),
    )(limit, asked, memory, memory, context, logs, grad)


def self_backward(rows, weight, limit, stored, grad, residual, causal):
    total, width = rows.shape
    pairs = width // PAIR
    block = min(256, total)
    queries, keys, values, attended, logs = stored

    def kernel(
        lim, x_ref, wq, wk, wv, q_ref, k_ref, v_ref, o_ref, l_ref, g_ref, r_ref,
        dx_ref, gq_ref, gk_ref, gv_ref, dxa, *scr,
    ):
        step = pl.program_id(0)
        attend_back_body(lim[0], q_ref, k_ref, v_ref, o_ref, l_ref, g_ref, scr, causal, block)
        dq = scr[4][...]
        dk = (scr[2][...] * (1.0 / LOG2E)).astype(BF16)
        dv = scr[3][...].astype(BF16)
        rows_in = x_ref[...]
        gq_ref[...] = tn(rows_in, dq).astype(BF16)
        gk_ref[...] = tn(rows_in, dk).astype(BF16)
        gv_ref[...] = tn(rows_in, dv).astype(BF16)
        packed = jnp.concatenate([dq, dk, dv], 1)
        weights = jnp.concatenate([wq[...], wk[...], wv[...]], 1)
        back = nt(packed, weights)

        @pl.when(step == 0)
        def _():
            dxa[...] = r_ref[...] + back

        @pl.when(step > 0)
        def _():
            dxa[...] += back

        @pl.when(step == pairs - 1)
        def _():
            dx_ref[...] = dxa[...]

    return pl.pallas_call(
        kernel,
        grid=(pairs,),
        in_specs=[smem(), whole(rows)]
        + [column(width, s * pairs) for s in range(3)]
        + [column(total)] * 6
        + [whole(residual)],
        out_specs=[whole(residual)] + [column(width)] * 3,
        out_shape=[jax.ShapeDtypeStruct((total, width), F32)]
        + [jax.ShapeDtypeStruct((width, width), BF16)] * 3,
        scratch_shapes=[pltpu.VMEM((total, width), F32)] + attend_scratch(total),
        compiler_params=params(),
    )(
        limit, rows, weight, weight, weight, queries, keys, values, attended, logs, grad, residual
    )


def row_block(block, width, last=None):
    if last is None:
        return pl.BlockSpec((block, width), lambda i: (i, 0))
    return pl.BlockSpec((block, width), lambda i: (jnp.minimum(i, last), 0))


def encoder_middle(attended, rows, weights, norms):
    out_weight, cross_weight, in_weight, down_weight = weights
    total, width = rows.shape
    hidden = in_weight.shape[1]
    block = min(256, total)

    def kernel(
        o_ref, x_ref, wo, wc, wi, wd, nr,
        y_ref, m_ref, n1_ref, r1_ref, n2_ref, r2_ref, f_ref, s_ref,
    ):
        source = x_ref[...].astype(F32)
        first, n1, r1 = norm_forward(source + nn(o_ref[...], wo[...]), nr[0:1, :], nr[2:3, :])
        active, slope = gelu_parts(nn(first.astype(BF16), wi[...]))
        active = active.astype(BF16)
        last, n2, r2 = norm_forward(first + nn(active, wd[...]) + source, nr[1:2, :], nr[3:4, :])
        y_ref[...] = last
        m_ref[...] = nn(last.astype(BF16), wc[...]).astype(BF16)
        n1_ref[...] = n1
        n2_ref[...] = n2
        r1_ref[...] = jnp.broadcast_to(r1, r1_ref.shape)
        r2_ref[...] = jnp.broadcast_to(r2, r2_ref.shape)
        f_ref[...] = active
        s_ref[...] = slope.astype(BF16)

    shapes = [
        (width, F32), (2 * width, BF16), (width, F32), (128, F32),
        (width, F32), (128, F32), (hidden, BF16), (hidden, BF16),
    ]
    return pl.pallas_call(
        kernel,
        grid=(total // block,),
        in_specs=[row_block(block, width)] * 2
        + [whole(a) for a in (out_weight, cross_weight, in_weight, down_weight, norms)],
        out_specs=[row_block(block, w) for w, _ in shapes],
        out_shape=[jax.ShapeDtypeStruct((total, w), d) for w, d in shapes],
        compiler_params=params(),
    )(attended, rows, out_weight, cross_weight, in_weight, down_weight, norms)


def decoder_middle(attended, rows, out_weight, cross_weight, norms):
    total, width = rows.shape
    block = min(256, total)

    def kernel(o_ref, x_ref, wo, wc, nr, q_ref, n1_ref, r1_ref):
        target = x_ref[...].astype(F32)
        first, n1, r1 = norm_forward(target + nn(o_ref[...], wo[...]), nr[0:1, :], nr[2:3, :])
        asked = nn(first.astype(BF16), wc[...])
        q_ref[...] = (asked * (SCALE * LOG2E)).astype(BF16)
        n1_ref[...] = n1
        r1_ref[...] = jnp.broadcast_to(r1, r1_ref.shape)

    half = pl.BlockSpec((width, width), lambda i: (0, 0), pipeline_mode=pl.Buffered(1))
    shapes = [(width, BF16), (width, F32), (128, F32)]
    return pl.pallas_call(
        kernel,
        grid=(total // block,),
        in_specs=[row_block(block, width)] * 2 + [whole(out_weight), half, whole(norms)],
        out_specs=[row_block(block, w) for w, _ in shapes],
        out_shape=[jax.ShapeDtypeStruct((total, w), d) for w, d in shapes],
        compiler_params=params(),
    )(attended, rows, out_weight, cross_weight, norms)


def add_rows(ref, step, grads):
    @pl.when(step == 0)
    def _():
        ref[...] = jnp.zeros_like(ref)

    for at, grad in enumerate(grads):
        ref[at : at + 1, :] += grad


def decoder_tail(context, n1, rows, seeds, weights, norms):
    cross_weight, in_weight, down_weight = weights
    total, width = rows.shape
    hidden = in_weight.shape[1]
    block = min(256, total)
    steps = total // block
    tiles = hidden // width

    def kernel(
        c_ref, n1_ref, x_ref, g_ref, wc, wi, wd, nr,
        y_ref, dl_ref, dm_ref, dc_ref, gi_ref, gd_ref, gc_ref, gn_ref,
        mixed_all, raised_all, active_all, down_all, mid_all, con_all,
    ):
        step = pl.program_id(0)

        @pl.when(step < steps)
        def _():
            here = pl.ds(pl.multiple_of(step * block, block), block)
            target = x_ref[...].astype(F32)
            first = n1_ref[...] * nr[0:1, :] + nr[2:3, :]
            mixed, nm, rm = norm_forward(first + nn(c_ref[...], wc[...]), nr[4:5, :], nr[5:6, :])
            mixed_low = mixed.astype(BF16)
            active, slope = gelu_parts(nn(mixed_low, wi[...]))
            active = active.astype(BF16)
            last, n2, r2 = norm_forward(mixed + nn(active, wd[...]) + target, nr[1:2, :], nr[3:4, :])
            y_ref[...] = last
            dlast, gain2, bias2 = norm_backward(g_ref[...].astype(F32), n2, r2, nr[1:2, :])
            down = dlast.astype(BF16)
            raised = (nt(down, wd[...]) * slope).astype(BF16)
            dmixed = dlast + nt(raised, wi[...])
            dmid, gainm, biasm = norm_backward(dmixed, nm, rm, nr[4:5, :])
            mid = dmid.astype(BF16)
            dl_ref[...] = dlast
            dm_ref[...] = dmid
            dc_ref[...] = nt(mid, wc[...]).astype(BF16)
            mixed_all[here, :] = mixed_low
            raised_all[here, :] = raised
            active_all[here, :] = active
            down_all[here, :] = down
            mid_all[here, :] = mid
            con_all[here, :] = c_ref[...]
            add_rows(gn_ref, step, (gain2, bias2, gainm, biasm))

        @pl.when(step >= steps)
        def _():
            tile = step - steps
            here = pl.ds(pl.multiple_of(tile * width, width), width)
            gi_ref[...] = tn(mixed_all[...], raised_all[:, here]).astype(BF16)
            gd_ref[...] = tn(active_all[:, here], down_all[...]).astype(BF16)

        @pl.when(step == steps)
        def _():
            gc_ref[...] = tn(con_all[...], mid_all[...]).astype(BF16)

    last_row = steps - 1
    half = pl.BlockSpec((width, width), lambda i: (0, 1), pipeline_mode=pl.Buffered(1))
    tile_at = lambda i: jnp.maximum(i - steps, 0)
    return pl.pallas_call(
        kernel,
        grid=(steps + tiles,),
        in_specs=[row_block(block, width, last_row)] * 4
        + [half, whole(in_weight), whole(down_weight), whole(norms)],
        out_specs=[row_block(block, width, last_row)] * 4
        + [
            pl.BlockSpec((width, width), lambda i: (0, tile_at(i))),
            pl.BlockSpec((width, width), lambda i: (tile_at(i), 0)),
            pl.BlockSpec((width, width), lambda i: (0, 0)),
            pl.BlockSpec((8, width), lambda i: (0, 0)),
        ],
        out_shape=[
            jax.ShapeDtypeStruct((total, width), F32),
            jax.ShapeDtypeStruct((total, width), F32),
            jax.ShapeDtypeStruct((total, width), F32),
            jax.ShapeDtypeStruct((total, width), BF16),
            jax.ShapeDtypeStruct((width, hidden), BF16),
            jax.ShapeDtypeStruct((hidden, width), BF16),
            jax.ShapeDtypeStruct((width, width), BF16),
            jax.ShapeDtypeStruct((8, width), F32),
        ],
        scratch_shapes=[
            pltpu.VMEM((total, width), BF16),
            pltpu.VMEM((total, hidden), BF16),
            pltpu.VMEM((total, hidden), BF16),
            pltpu.VMEM((total, width), BF16),
            pltpu.VMEM((total, width), BF16),
            pltpu.VMEM((total, width), BF16),
        ],
        compiler_params=params(),
    )(context, n1, rows, seeds, cross_weight, in_weight, down_weight, norms)


def encoder_back(dkeys, dvalues, attended, kept, weights, norms):
    out_weight, cross_weight, in_weight, down_weight = weights
    n1, r1, n2, r2, active, slope = kept
    total, width = n1.shape
    hidden = in_weight.shape[1]
    block = min(256, total)
    steps = total // block
    tiles = hidden // width

    def kernel(
        dk_ref, dv_ref, o_ref, n1_ref, r1_ref, n2_ref, r2_ref, f_ref, s_ref, wo, wc, wi, wd, nr,
        da_ref, res_ref, gi_ref, gd_ref, gc_ref, go_ref, gn_ref,
        hid_all, raised_all, active_all, down_all, first_all, att_all, last_all, dk_all, dv_all,
    ):
        step = pl.program_id(0)

        @pl.when(step < steps)
        def _():
            here = pl.ds(pl.multiple_of(step * block, block), block)
            dk, dv = dk_ref[...], dv_ref[...]
            n1_rows, n2_rows = n1_ref[...], n2_ref[...]
            dy = nt(dk, wc[:, :width]) + nt(dv, wc[:, width:])
            dlast, gain2, bias2 = norm_backward(dy, n2_rows, r2_ref[:, 0:1], nr[1:2, :])
            down = dlast.astype(BF16)
            raised = (nt(down, wd[...]) * s_ref[...].astype(F32)).astype(BF16)
            dhidden = dlast + nt(raised, wi[...])
            dfirst, gain1, bias1 = norm_backward(dhidden, n1_rows, r1_ref[:, 0:1], nr[0:1, :])
            first = dfirst.astype(BF16)
            da_ref[...] = nt(first, wo[...]).astype(BF16)
            res_ref[...] = dlast + dfirst
            hid_all[here, :] = (n1_rows * nr[0:1, :] + nr[2:3, :]).astype(BF16)
            last_all[here, :] = (n2_rows * nr[1:2, :] + nr[3:4, :]).astype(BF16)
            raised_all[here, :] = raised
            active_all[here, :] = f_ref[...]
            down_all[here, :] = down
            first_all[here, :] = first
            att_all[here, :] = o_ref[...]
            dk_all[here, :] = dk
            dv_all[here, :] = dv
            add_rows(gn_ref, step, (gain1, gain2, bias1, bias2))

        @pl.when(step >= steps)
        def _():
            tile = step - steps
            here = pl.ds(pl.multiple_of(tile * width, width), width)
            gi_ref[...] = tn(hid_all[...], raised_all[:, here]).astype(BF16)
            gd_ref[...] = tn(active_all[:, here], down_all[...]).astype(BF16)

        @pl.when(step == steps)
        def _():
            gc_ref[:, :width] = tn(last_all[...], dk_all[...]).astype(BF16)
            gc_ref[:, width:] = tn(last_all[...], dv_all[...]).astype(BF16)
            go_ref[...] = tn(att_all[...], first_all[...]).astype(BF16)

    last_row = steps - 1
    row = row_block(block, width, last_row)
    thin = row_block(block, 128, last_row)
    wide = row_block(block, hidden, last_row)
    tile_at = lambda i: jnp.maximum(i - steps, 0)
    return pl.pallas_call(
        kernel,
        grid=(steps + tiles,),
        in_specs=[row] * 3
        + [row, thin, row, thin, wide, wide]
        + [whole(a) for a in (out_weight, cross_weight, in_weight, down_weight, norms)],
        out_specs=[row] * 2
        + [
            pl.BlockSpec((width, width), lambda i: (0, tile_at(i))),
            pl.BlockSpec((width, width), lambda i: (tile_at(i), 0)),
            pl.BlockSpec((width, 2 * width), lambda i: (0, 0)),
            pl.BlockSpec((width, width), lambda i: (0, 0)),
            pl.BlockSpec((8, width), lambda i: (0, 0)),
        ],
        out_shape=[
            jax.ShapeDtypeStruct((total, width), BF16),
            jax.ShapeDtypeStruct((total, width), F32),
            jax.ShapeDtypeStruct((width, hidden), BF16),
            jax.ShapeDtypeStruct((hidden, width), BF16),
            jax.ShapeDtypeStruct((width, 2 * width), BF16),
            jax.ShapeDtypeStruct((width, width), BF16),
            jax.ShapeDtypeStruct((8, width), F32),
        ],
        scratch_shapes=[
            pltpu.VMEM((total, width), BF16),
            pltpu.VMEM((total, hidden), BF16),
            pltpu.VMEM((total, hidden), BF16),
        ]
        + [pltpu.VMEM((total, width), BF16)] * 6,
        compiler_params=params(),
    )(
        dkeys, dvalues, attended, n1, r1, n2, r2, active, slope,
        out_weight, cross_weight, in_weight, down_weight, norms,
    )


def decoder_back(dasked, dmid, dlast, attended, n1, r1, out_weight, cross_weight, norms):
    total, width = n1.shape
    block = min(256, total)
    steps = total // block

    def kernel(
        dq_ref, dm_ref, dl_ref, o_ref, n1_ref, r1_ref, wo, wc, nr,
        da_ref, res_ref, gc_ref, go_ref, gn_ref, hid_all, first_all, att_all, dq_all,
    ):
        step = pl.program_id(0)
        here = pl.ds(pl.multiple_of(step * block, block), block)
        dq = dq_ref[...]
        n1_rows = n1_ref[...]
        dhidden = dm_ref[...] + nt(dq, wc[...])
        dfirst, gain1, bias1 = norm_backward(dhidden, n1_rows, r1_ref[:, 0:1], nr[0:1, :])
        first = dfirst.astype(BF16)
        da_ref[...] = nt(first, wo[...]).astype(BF16)
        res_ref[...] = dl_ref[...] + dfirst
        hid_all[here, :] = (n1_rows * nr[0:1, :] + nr[2:3, :]).astype(BF16)
        first_all[here, :] = first
        att_all[here, :] = o_ref[...]
        dq_all[here, :] = dq
        add_rows(gn_ref, step, (gain1, bias1))

        @pl.when(step == steps - 1)
        def _():
            gc_ref[...] = tn(hid_all[...], dq_all[...]).astype(BF16)
            go_ref[...] = tn(att_all[...], first_all[...]).astype(BF16)

    row = row_block(block, width)
    half = pl.BlockSpec((width, width), lambda i: (0, 0), pipeline_mode=pl.Buffered(1))
    square = pl.BlockSpec((width, width), lambda i: (0, 0))
    return pl.pallas_call(
        kernel,
        grid=(steps,),
        in_specs=[row] * 5 + [row_block(block, 128), whole(out_weight), half, whole(norms)],
        out_specs=[row] * 2 + [square, square, pl.BlockSpec((8, width), lambda i: (0, 0))],
        out_shape=[
            jax.ShapeDtypeStruct((total, width), BF16),
            jax.ShapeDtypeStruct((total, width), F32),
            jax.ShapeDtypeStruct((width, width), BF16),
            jax.ShapeDtypeStruct((width, width), BF16),
            jax.ShapeDtypeStruct((8, width), F32),
        ],
        scratch_shapes=[pltpu.VMEM((total, width), BF16)] * 4,
        compiler_params=params(),
    )(dasked, dmid, dlast, attended, n1, r1, out_weight, cross_weight, norms)


def local(
    inputs,
    lengths,
    cotangent,
    qkv_weight,
    out_weight,
    cross_weight,
    ffn_in,
    ffn_out,
    norm_gain,
    norm_bias,
    cross_norm,
):
    section = lax.axis_index("section")
    first = section == 0
    swap = [(0, 1), (1, 0)]

    def swapped(value):
        return lax.ppermute(value, "section", swap)

    def pick(value, at):
        return lax.dynamic_index_in_dim(value, at, 0, keepdims=False)

    def both(own):
        other = swapped(own)
        return jnp.where(first, own, other), jnp.where(first, other, own)

    def share(value):
        own, other = pick(value, section), swapped(pick(value, 1 - section))
        return jnp.where(first, own, other), jnp.where(first, other, own)

    source, target = share(inputs[0])
    source_limit, target_limit = share(lengths[0][:, None])
    seeds = pick(cotangent, section)
    enc_qkv, dec_qkv = both(qkv_weight[0])
    enc_out, dec_out = both(out_weight[0])
    enc_cross, dec_cross = both(cross_weight[0])
    enc_in, dec_in = both(ffn_in[0])
    enc_down, dec_down = both(ffn_out[0])
    enc_norm, dec_norm = both(jnp.concatenate([norm_gain[0], norm_bias[0]], 0))
    width = source.shape[1]
    empty = jnp.zeros((2, width), F32)
    enc_norm = jnp.concatenate([enc_norm, empty, empty], 0)
    dec_norm = jnp.concatenate([dec_norm, cross_norm, empty], 0)

    enc_self = self_forward(source, enc_qkv, source_limit, False)
    dec_self = self_forward(target, dec_qkv, target_limit, True)
    enc_weights = (enc_out, enc_cross, enc_in, enc_down)
    enc_rows, memory, *enc_kept = encoder_middle(enc_self[3], source, enc_weights, enc_norm)
    asked, dec_n1, dec_r1 = decoder_middle(dec_self[3], target, dec_out, dec_cross, dec_norm)
    context, cross_logs = cross_forward(asked, memory, source_limit)
    dec_rows, dec_last, dec_mid, dcontext, dec_gi, dec_gd, dec_gco, dec_gn = decoder_tail(
        context, dec_n1, target, seeds, (dec_cross, dec_in, dec_down), dec_norm
    )
    every = ("section", "dp")
    dec_gi, dec_gd, dec_gco, dec_gn = lax.psum(
        (dec_gi, dec_gd, dec_gco, dec_gn.astype(BF16)), every
    )
    dasked, dkeys, dvalues = cross_backward(
        asked, memory, source_limit, context, cross_logs, dcontext
    )
    denc, enc_res, enc_gi, enc_gd, enc_gc, enc_go, enc_gn = encoder_back(
        dkeys, dvalues, enc_self[3], enc_kept, enc_weights, enc_norm
    )
    ddec, dec_res, dec_gcq, dec_go, dec_gn1 = decoder_back(
        dasked, dec_mid, dec_last, dec_self[3], dec_n1, dec_r1, dec_out, dec_cross, dec_norm
    )
    enc_dx, *enc_gqkv = self_backward(
        source, enc_qkv, source_limit, enc_self, denc, enc_res, False
    )
    dec_dx, *dec_gqkv = self_backward(
        target, dec_qkv, target_limit, dec_self, ddec, dec_res, True
    )
    send = tuple(
        jnp.where(first, d, e)
        for d, e in zip(
            [*dec_gqkv, dec_go, dec_gcq, dec_gn1.astype(BF16)],
            [*enc_gqkv, enc_go, enc_gc[:, :width], enc_gn.astype(BF16)],
        )
    )
    keep = tuple(
        jnp.where(first, e, d)
        for d, e in zip(
            [*dec_gqkv, dec_go, dec_gcq, dec_gn1.astype(BF16)],
            [*enc_gqkv, enc_go, enc_gc[:, :width], enc_gn.astype(BF16)],
        )
    )
    enc_gi, enc_gd, enc_gcv = lax.psum((enc_gi, enc_gd, enc_gc[:, width:]), every)
    mine = lax.psum(tuple(k + s for k, s in zip(keep, swapped(send))), "dp")

    def choose(e, d):
        return jnp.where(first, e, d).astype(F32)[None]

    def spread(e, d):
        own, other = jnp.where(first, e, d), swapped(jnp.where(first, d, e))
        low, high = jnp.where(first, own, other), jnp.where(first, other, own)
        return jnp.stack([low, high])[None]

    norm_own = mine[5].astype(F32)
    norm_dec = dec_gn.astype(F32)
    gains = jnp.where(first, norm_own[0:2], jnp.stack([norm_own[0], norm_dec[0]]))
    biases = jnp.where(first, norm_own[2:4], jnp.stack([norm_own[1], norm_dec[1]]))
    cross_row = jnp.where(first, norm_dec[2], norm_dec[3])
    return (
        spread(enc_rows, dec_rows),
        spread(enc_dx, dec_dx),
        jnp.concatenate(mine[:3], 1).astype(F32)[None],
        mine[3].astype(F32)[None],
        jnp.concatenate([mine[4], jnp.where(first, enc_gcv, dec_gco)], 1).astype(F32)[None],
        choose(enc_gi, dec_gi),
        choose(enc_gd, dec_gd),
        gains[None],
        biases[None],
        cross_row[None],
    )


def solution(mesh):
    in_specs = (
        P("section", "dp", None, None),
        P("section", "dp"),
        P("dp", None, None),
        P("section", None, None),
        P("section", None, None),
        P("section", None, None),
        P("section", None, None),
        P("section", None, None),
        P("section", None, None),
        P("section", None, None),
        P(),
    )
    out_specs = (
        P("section", "dp", None, None),
        P("section", "dp", None, None),
        P("section", None, None),
        P("section", None, None),
        P("section", None, None),
        P("section", None, None),
        P("section", None, None),
        P("section", None, None),
        P("section", None, None),
        P("section", None),
    )
    return jax.shard_map(local, mesh=mesh, in_specs=in_specs, out_specs=out_specs, check_vma=False)
```

time: 2240 us -> 630 us (0.28)
  waiting for transfers between devices: 1260 us -> 234 us
  matrix products: 544 us -> 0 us
  Pallas kernels: 0 us -> 215 us
  local copies, waits for them, and re-layouts: 177 us -> 8.47 us
  other arithmetic: 142 us -> 54.1 us
    ppermute x4 -> x16, waiting for transfers between devices: 948 us -> 3.8 us  [swapped(): return lax.ppermute(value, 'section', swap)]
    dot_general x72 -> x0, matrix products: 544 us -> none  [the longest x16 115 us: product(): return jnp.dot(left_side, right_side, preferred_element_type=jnp.float32)]
    pallas_call x0 -> x11, Pallas kernels: none -> 215 us  [the longest x2 59.3 us: self_backward(): pl.pallas_call(kernel, grid=(pairs,), in_specs=[smem(), whole(rows)] + [c...]
    psum x1 -> x2, waiting for transfers between devices: 310 us -> 230 us  [the longest x1 193 us: local(): lax.psum((enc_gi, enc_gd, enc_gc[:, width:]), every)]
    sub x4 -> x0, other arithmetic: 76.2 us -> none  [one_block(): exp_scores = jnp.exp(scores - row_peak)]
    while x172 -> x0, local copies, waits for them, and re-layouts: 52.9 us -> none
    cond x5 -> x0, local copies, waits for them, and re-layouts: 25.5 us -> none  [the longest x4 19.3 us: local(): lax.cond(first_section, decode_spare, decode_all)]
    slice x18 -> x2, local copies, waits for them, and re-layouts: 25.3 us -> 0.01 us  [the longest x1 0.01 us: local(): norm_own[1]]
  transfers between devices with their start and end apart: 5 -> 18, of which waited for: 4 -> 4; matrix products, arithmetic and copies ran while one was open for 1% -> 7% of each run, Pallas kernels for 0% -> 16%
where the time goes in v1:
time: 630 us; the launch traced here: 621 us
  waiting for transfers between devices  234 us (37%)
  Pallas kernels  215 us (34%)
  blocking collectives  84.5 us (13%)
  other arithmetic  54.1 us (9%)
  between operations  17.2 us (3%)
  local copies, waits for them, and re-layouts  8.47 us (1%)
  starting transfers between devices  7.29 us (1%)
    psum x1, waiting for transfers between devices, local(): lax.psum((enc_gi, enc_gd, enc_gc[:, width:]), every)  193 us
    pallas_call x2, Pallas kernels, self_backward(): pl.pallas_call(kernel, grid=(pairs,), in_specs=[smem(), whole(rows)] + [c...  59.3 us
    psum x1, blocking collectives, local(): lax.psum((dec_gi, dec_gd, dec_gco, dec_gn.astype(BF16)), every)  43.3 us
    psum x1, blocking collectives, local(): mine = lax.psum(tuple((k + s for k, s in zip(keep, swapped(send)))), 'dp')  41.2 us
    psum x1, waiting for transfers between devices, local(): mine = lax.psum(tuple((k + s for k, s in zip(keep, swapped(send)))), 'dp')  36.8 us
    pallas_call x2, Pallas kernels, self_forward(): pl.pallas_call(kernel, grid=(pairs,), in_specs=[smem(), whole(rows)] + [c...  36.4 us
    pallas_call x1, Pallas kernels, decoder_tail(): pl.pallas_call(kernel, grid=(steps + tiles,), in_specs=[row_block(block,...  26.9 us
    pallas_call x1, Pallas kernels, cross_backward(): pl.pallas_call(kernel, grid=(pairs,), in_specs=[smem(), column(total), co...  24.9 us
  transfers between devices with their start and end apart: 18, of which 4 were waited for; matrix products, arithmetic and copies ran while one was open for 7% of the time, Pallas kernels for 16%

profile of v1, /device:TPU:0, one launch (start us, length us, event | category | flops | bytes accessed | tf_op | source)
XLA Modules:
  0.0 620.7 jit_solution(4570150472414420312)
XLA Ops:
  7.3 2.4 dynamic-slice_bitcast_fusion.1
  9.7 0.5 collective-permute-start.1
  10.2 0.5 collective-permute-start.7
  10.8 0.6 constant_dynamic-slice_fusion
  11.4 0.5 collective-permute-start.3
  11.9 3.2 collective-permute-done
  15.1 0.4 collective-permute-start.4
  15.4 0.1 collective-permute-start.6
  15.6 1.1 dynamic-slice_bitcast_fusion.g_ref
  19.3 0.6 concatenate.41.nr
  19.9 0.7 maximum_maximum_fusion.nr
  20.6 0.4 collective-permute-start.5
  20.9 2.2 broadcast_select_fusion.18
  23.2 3.0 bitcast_select_fusion.1
  26.2 2.7 broadcast_select_fusion.7
  28.9 3.8 broadcast_select_fusion.5
  32.7 18.7 %shard_map.186 = (bf16[1024,512]{1,0:T(8,128)(2,1)}, bf16[1024,512]{1,0:T(8,128)(2,1)}, bf16[1024,512]{1,0:T(8,128)(2,1)}, bf16[1024,512]{1,0:T(8,128)(2,1)}, f32[1024,512]{1,0:T(8,128)}) custom-call(s32[1]{0:T(128)S(6)} %select_n.230.lim, bf16[1024,512]{1,0:T(8,128)(2,1)} %get-tuple-element.139.x_ref, bf16[512,1536]{1,0:T(8,128)(2,1)} %get-tuple-element.137.wq.wk.wv, ...), custom_call_target="tpu_custom_call" | custom-call | tf_op jit(solution)/shard_map/pallas_call | solution.py:202
  51.4 17.7 %shard_map.188 = (bf16[1024,512]{1,0:T(8,128)(2,1)}, bf16[1024,512]{1,0:T(8,128)(2,1)}, bf16[1024,512]{1,0:T(8,128)(2,1)}, bf16[1024,512]{1,0:T(8,128)(2,1)}, f32[1024,512]{1,0:T(8,128)}) custom-call(s32[1]{0:T(128)S(6)} %select_n.244.lim, bf16[1024,512]{1,0:T(8,128)(2,1)} %get-tuple-element.140.x_ref, bf16[512,1536]{1,0:T(8,128)(2,1)} %get-tuple-element.138.wq.wk.wv, ...), custom_call_target="tpu_custom_call" | custom-call | tf_op jit(solution)/shard_map/pallas_call | solution.py:202
  69.1 5.6 shard_map.189
  74.8 4.0 broadcast_select_fusion
  78.8 2.5 broadcast_select_fusion.2
  81.3 14.9 %shard_map.187 = (f32[1024,512]{1,0:T(8,128)}, bf16[1024,1024]{1,0:T(8,128)(2,1)}, f32[1024,512]{1,0:T(8,128)}, f32[1024,128]{1,0:T(8,128)}, f32[1024,512]{1,0:T...) custom-call(bf16[1024,512]{1,0:T(8,128)(2,1)} %get-tuple-element.64.o_ref, ...), custom_call_target="tpu_custom_call" | custom-call | tf_op jit(solution)/shard_map/pallas_call | solution.py:344
  96.2 14.2 %shard_map.190 = (bf16[1024,512]{1,0:T(8,128)(2,1)}, f32[1024,512]{1,0:T(8,128)}) custom-call(s32[1]{0:T(128)S(6)} %select_n.230.lim, bf16[1024,512]{1,0:T(8,128)(2,1)} %get-tuple-element.67.q_ref, bf16[1024,1024]{1,0:T(8,128)(2,1)} %get-tuple-element.68.k_ref.v_ref, bf16[1024,1024]{1,0:T(8,128)(2,1)} %get-tuple-element.68.k_ref.v_ref), custom_call_target="tpu_custom_call" | custom-call | tf_op jit(solution)/shard_map/pallas_call | solution.py:222
  110.5 26.9 %shard_map.191 = (f32[1024,512]{1,0:T(8,128)}, f32[1024,512]{1,0:T(8,128)}, f32[1024,512]{1,0:T(8,128)}, bf16[1024,512]{1,0:T(8,128)(2,1)}, bf16[512,2048]{1,0:T...) custom-call(bf16[1024,512]{1,0:T(8,128)(2,1)} %get-tuple-element.69.c_ref.o_ref, ...), custom_call_target="tpu_custom_call" | custom-call | tf_op jit(solution)/shard_map/pallas_call | solution.py:445
  137.4 24.9 %shard_map.192 = (bf16[1024,512]{1,0:T(8,128)(2,1)}, bf16[1024,512]{1,0:T(8,128)(2,1)}, bf16[1024,512]{1,0:T(8,128)(2,1)}) custom-call(s32[1]{0:T(128)S(6)} %select_n.230.lim, bf16[1024,512]{1,0:T(8,128)(2,1)} %get-tuple-element.67.q_ref, bf16[1024,1024]{1,0:T(8,128)(2,1)} %get-tuple-element.68.k_ref.v_ref, ...), custom_call_target="tpu_custom_call" | custom-call | tf_op jit(solution)/shard_map/pallas_call | solution.py:247
  162.3 9.3 %shard_map.195 = (bf16[1024,512]{1,0:T(8,128)(2,1)}, f32[1024,512]{1,0:T(8,128)}, bf16[512,512]{1,0:T(8,128)(2,1)}, bf16[512,512]{1,0:T(8,128)(2,1)}, f32[8,512]{1,0:T(8,128)}) custom-call(bf16[1024,512]{1,0:T(8,128)(2,1)} %get-tuple-element.93.dq_ref, f32[1024,512]{1,0:T(8,128)} %get-tuple-element.94.dm_ref, f32[1024,512]{1,0:T(8,128)} %get-tuple-element.95.dl_ref, ...), custom_call_target="tpu_custom_call" | custom-call | tf_op jit(solution)/shard_map/pallas_call | solution.py:606
  171.7 23.3 %shard_map.193 = (bf16[1024,512]{1,0:T(8,128)(2,1)}, f32[1024,512]{1,0:T(8,128)}, bf16[512,2048]{1,0:T(8,128)(2,1)}, bf16[2048,512]{1,0:T(8,128)(2,1)}, bf16[512...) custom-call(bf16[1024,512]{1,0:T(8,128)(2,1)} %get-tuple-element.78.dk_ref, ...), custom_call_target="tpu_custom_call" | custom-call | tf_op jit(solution)/shard_map/pallas_call | solution.py:538
  195.1 1.2 collective-permute-start.13
  196.3 26.5 %shard_map.196 = (f32[1024,512]{1,0:T(8,128)}, bf16[512,512]{1,0:T(8,128)(2,1)}, bf16[512,512]{1,0:T(8,128)(2,1)}, bf16[512,512]{1,0:T(8,128)(2,1)}) custom-call(s32[1]{0:T(128)S(6)} %select_n.244.lim, bf16[1024,512]{1,0:T(8,128)(2,1)} %get-tuple-element.140.x_ref, bf16[512,1536]{1,0:T(8,128)(2,1)} %get-tuple-element.138.wq.wk.wv, ...), custom_call_target="tpu_custom_call" | custom-call | tf_op jit(solution)/shard_map/pallas_call | solution.py:293
  222.8 32.9 %shard_map.194 = (f32[1024,512]{1,0:T(8,128)}, bf16[512,512]{1,0:T(8,128)(2,1)}, bf16[512,512]{1,0:T(8,128)(2,1)}, bf16[512,512]{1,0:T(8,128)(2,1)}) custom-call(s32[1]{0:T(128)S(6)} %select_n.230.lim, bf16[1024,512]{1,0:T(8,128)(2,1)} %get-tuple-element.139.x_ref, bf16[512,1536]{1,0:T(8,128)(2,1)} %get-tuple-element.137.wq.wk.wv, ...), custom_call_target="tpu_custom_call" | custom-call | tf_op jit(solution)/shard_map/pallas_call | solution.py:293
  255.8 1.3 collective-permute-start.12
  257.1 1.1 collective-permute-start.11
  258.5 0.9 fusion.2
  259.3 0.5 collective-permute-start.14
  259.8 0.9 add_bitcast_fusion.1
  260.7 0.9 add_bitcast_fusion.2
  261.6 0.9 add_bitcast_fusion.3
  262.4 0.9 add_bitcast_fusion.4
  263.4 0.9 add_bitcast_fusion
  264.3 0.7 all-reduce.6.cloned.1.call-update
  265.0 0.9 copy-done.2
  265.9 3.6 broadcast_select_fusion.10
  269.5 1.8 broadcast_select_fusion.8
  271.3 0.5 collective-permute-start.9
  271.8 43.3 %psum.103 = bf16[8,512]{1,0:T(8,128)(2,1)S(1)} all-reduce(bf16[8,512]{1,0:T(8,128)(2,1)S(1)} %convert_element_type.45), channel_id=1, replica_groups=mesh['section'=2,'dp'=16] {'section','dp'}, use_global_device_ids=true, to_apply=%region_12.13 | all-reduce | flops 4096 | bytes 16384 | tf_op jit(solution)/shard_map/psum | solution.py:678
  315.2 0.6 broadcast_select_fusion.20
  315.8 0.6 collective-permute-done.15
  316.3 41.2 %psum.102 = bf16[8,512]{1,0:T(8,128)(2,1)S(1)} all-reduce(bf16[8,512]{1,0:T(8,128)(2,1)S(1)} %select_add_fusion), channel_id=1, replica_groups=mesh['section'=2,'dp'=16] {'dp'}, use_global_device_ids=true, to_apply=%region_11.12 | all-reduce | flops 4096 | bytes 16384 | tf_op jit(solution)/shard_map/psum | solution.py:711
  357.6 0.6 fusion
  358.2 2.4 select_bitcast_fusion.3
  360.7 2.6 maximum_bitcast_fusion
  363.2 1.2 copy-done.6
  364.4 2.4 select_bitcast_fusion.1
  366.8 2.5 maximum_bitcast_fusion.1
  369.3 36.8 %all-reduce.8.cloned.1.call-done = (bf16[1,512,512]{2,1,0:T(8,128)(2,1)}, bf16[1,512,512]{2,1,0:T(8,128)(2,1)}, bf16[1,512,512]{2,1,0:T(8,128)(2,1)}, bf16[1,512,512]{2,1,0:T(8,128)(2,1)}, bf16[1,512,512]{2,1,0:T(8,128)(2,1)}) async-done(((bf16[1,512,512]{2,1,0:T(8,128)(2,1)}, bf16[1,512,512]{2,1,0:T(8,128)(2,1)}, bf16[1,512,512]{2,1,0:T(8,128)(2,1)}, bf16[1,512,512]{2,1,0:T(8,128)(2,1)}, ...) | async-done | bytes 2621456 | tf_op jit(solution)/shard_map/psum | solution.py:711
  406.1 2.1 broadcast_in_dim.40
  408.2 3.5 maximum_convert_fusion
  411.7 192.8 %all-reduce.6.cloned.1.call-done = (bf16[512,512]{1,0:T(8,128)(2,1)}, bf16[512,512]{1,0:T(8,128)(2,1)}, bf16[512,2048]{1,0:T(8,128)(2,1)}, bf16[512,2048]{1,0:T(...) async-done(((bf16[512,512]{1,0:T(8,128)(2,1)}, bf16[512,512]{1,0:T(8,128)(2,1)}, bf16[512,2048]{1,0:T(8,128)(2,1)}, bf16[512,2048]{1,0:T(8,128)(2,1)}, ...) | async-done | bytes 9437200 | tf_op jit(solution)/shard_map/psum | solution.py:710
  604.6 1.2 select_bitcast_fusion.4
  605.8 1.6 maximum_convert_fusion.1
  607.4 2.4 bitcast_convert_fusion.1
  609.8 1.3 copy-done.20
  611.2 2.3 bitcast_convert_fusion
  613.4 0.2 copy-done.1
  (97 shorter events, 0.9 us)
Async XLA Ops:
  7.2 8.4 %copy-start = (bf16[2,1024,512]{2,1,0:T(8,128)(2,1)S(1)}, bf16[2,1024,512]{2,1,0:T(8,128)(2,1)}, u32[]{:S(2)}) copy-start(bf16[2,1024,512]{2,1,0:T(8,128)(2,1)} %param.13) | copy-start | bytes 6291460
  7.2 3.0 copy-start.28
  7.2 3.0 copy-start.29
  7.2 3.5 copy-start.31
  7.2 7.8 %copy-start.23 = (bf16[1,512,1024]{2,1,0:T(8,128)(2,1)S(1)}, bf16[1,512,1024]{2,1,0:T(8,128)(2,1)}, u32[]{:S(2)}) copy-start(bf16[1,512,1024]{2,1,0:T(8,128)(2,1)} %param.16) | copy-start | bytes 3145732
  7.2 398.9 %all-reduce.8.cloned.1.call-start = ((), (), s32[]{:S(2)}) async-start(), calls=%async_computation.1 | async-start | bytes 5242880 | tf_op jit(solution)/shard_map/psum | solution.py:711
  7.3 12.6 %copy-start.30 = (f32[2,512]{1,0:T(2,128)S(1)}, f32[2,512]{1,0:T(2,128)}, u32[]{:S(2)}) copy-start(f32[2,512]{1,0:T(2,128)} %param.21) | copy-start | bytes 12292
  9.7 13.5 %collective-permute-start.1 = (bf16[1024,512]{1,0:T(8,128)(2,1)}, bf16[1024,512]{1,0:T(8,128)(2,1)}, u32[]{:S(2)}, u32[]{:S(2)}) collective-permute-start(bf16[1024,512]{1,0:T(8,128)(2,1)} %dynamic-slice_bitcast_fusion.1), channel_id=1, source_target_pairs={{0,16},{16,0},{1,17},{17,1},{2,18},{18,2},{3,19},{19,3},{4,20},{20... | collective-permute-start | bytes 3145736 | tf_op jit(solution)/shard_map/ppermute | solution.py:641
  10.2 18.7 %collective-permute-start.2 = (bf16[512,1536]{1,0:T(8,128)(2,1)}, bf16[512,1536]{1,0:T(8,128)(2,1)}, u32[]{:S(2)}, u32[]{:S(2)}) collective-permute-start(bf16[512,1536]{1,0:T(8,128)(2,1)} %bitcast.5), channel_id=1, source_target_pairs={{0,16},{16,0},{1,17},{17,1},{2,18},{18,2},{3,19},{19,3},{4,20},{20... | collective-permute-start | bytes 4718600 | tf_op jit(solution)/shard_map/ppermute | solution.py:641
  10.2 5.2 collective-permute-start.7
  11.3 3.7 collective-permute-start
  11.4 9.2 %collective-permute-start.3 = (bf16[512,512]{1,0:T(8,128)(2,1)}, bf16[512,512]{1,0:T(8,128)(2,1)}, u32[]{:S(2)}, u32[]{:S(2)}) collective-permute-start(bf16[512,512]{1,0:T(8,128)(2,1)} %bitcast.64), channel_id=1, source_target_pairs={{0,16},{16,0},{1,17},{17,1},{2,18},{18,2},{3,19},{19,3},{4,20},{20... | collective-permute-start | bytes 1572872 | tf_op jit(solution)/shard_map/ppermute | solution.py:641
  15.1 11.1 %collective-permute-start.4 = (bf16[512,1024]{1,0:T(8,128)(2,1)S(1)}, bf16[512,1024]{1,0:T(8,128)(2,1)}, u32[]{:S(2)}, u32[]{:S(2)}) collective-permute-start(bf16[512,1024]{1,0:T(8,128)(2,1)S(1)} %bitcast.63), channel_id=1, source_target_pairs={{0,16},{16,0},{1,17},{17,1},{2,18},{18,2},{3,19},{19,3},{4,20},{20... | collective-permute-start | bytes 3145736 | tf_op jit(solution)/shard_map/ppermute | solution.py:641
  15.4 59.3 %collective-permute-start.6 = (bf16[2048,512]{1,0:T(8,128)(2,1)}, bf16[2048,512]{1,0:T(8,128)(2,1)}, u32[]{:S(2)}, u32[]{:S(2)}) collective-permute-start(bf16[2048,512]{1,0:T(8,128)(2,1)} %bitcast.61), channel_id=1, source_target_pairs={{0,16},{16,0},{1,17},{17,1},{2,18},{18,2},{3,19},{19,3},{4,20},{20... | collective-permute-start | bytes 6291464 | tf_op jit(solution)/shard_map/ppermute | solution.py:641
  20.6 58.2 %collective-permute-start.5 = (bf16[512,2048]{1,0:T(8,128)(2,1)}, bf16[512,2048]{1,0:T(8,128)(2,1)S(1)}, u32[]{:S(2)}, u32[]{:S(2)}) collective-permute-start(bf16[512,2048]{1,0:T(8,128)(2,1)} %bitcast.62), channel_id=1, source_target_pairs={{0,16},{16,0},{1,17},{17,1},{2,18},{18,2},{3,19},{19,3},{4,20},{20... | collective-permute-start | bytes 6291464 | tf_op jit(solution)/shard_map/ppermute | solution.py:641
  69.1 5.7 copy-start.17
  74.8 4.0 copy-start.18
  171.7 23.3 %copy-start.8 = (bf16[512,512]{1,0:T(8,128)(2,1)S(1)}, bf16[512,512]{1,0:T(8,128)(2,1)}, u32[]{:S(2)}) copy-start(bf16[512,512]{1,0:T(8,128)(2,1)} %get-tuple-element.107) | copy-start | bytes 1572868
  195.1 64.7 %collective-permute-start.13 = (bf16[512,512]{1,0:T(8,128)(2,1)S(1)}, bf16[512,512]{1,0:T(8,128)(2,1)S(1)}, u32[]{:S(2)}, u32[]{:S(2)}) collective-permute-start(bf16[512,512]{1,0:T(8,128)(2,1)S(1)} %broadcast_select_fusion.13), channel_id=1, source_target_pairs={{0,16},{16,0},{1,17},{17,1},{2,18},{18,2},{3,19},{19,3},{4,20},{20... | collective-permute-start | bytes 1572872 | tf_op jit(solution)/shard_map/ppermute | solution.py:641
  222.8 32.9 %copy-start.12 = (bf16[512,512]{1,0:T(8,128)(2,1)S(1)}, bf16[512,512]{1,0:T(8,128)(2,1)}, u32[]{:S(2)}) copy-start(bf16[512,512]{1,0:T(8,128)(2,1)} %get-tuple-element.105) | copy-start | bytes 1572868
  222.8 34.3 %copy-start.11 = (bf16[512,512]{1,0:T(8,128)(2,1)S(1)}, bf16[512,512]{1,0:T(8,128)(2,1)}, u32[]{:S(2)}) copy-start(bf16[512,512]{1,0:T(8,128)(2,1)} %get-tuple-element.103) | copy-start | bytes 1572868
  255.7 2.6 copy-start.10
  255.7 2.6 copy-start.13
  255.7 2.8 copy-start.7
  255.7 2.8 copy-start.16
  255.8 4.9 collective-permute-start.12
  257.1 4.4 collective-permute-start.11
  258.3 1.5 copy-start.9
  258.3 4.1 collective-permute-start.10
  258.5 2.2 copy-start.15
  259.3 2.2 copy-start.14
  259.3 4.0 collective-permute-start.14
  264.3 340.3 %all-reduce.6.cloned.1.call-start = ((), (), s32[]{:S(2)}) async-start(), calls=%async_computation | async-start | bytes 18874368 | tf_op jit(solution)/shard_map/psum | solution.py:710
  264.3 1.6 copy-start.2
  265.9 3.6 copy-start.3
  265.9 3.6 copy-start.5
  269.5 88.7 %collective-permute-start.8 = (f32[1024,512]{1,0:T(8,128)}, f32[1024,512]{1,0:T(8,128)}, u32[]{:S(2)}, u32[]{:S(2)}) collective-permute-start(f32[1024,512]{1,0:T(8,128)} %broadcast_select_fusion.10), channel_id=1, source_target_pairs={{0,16},{16,0},{1,17},{17,1},{2,18},{18,2},{3,19},{19,3},{4,20},{20... | collective-permute-start | bytes 6291464 | tf_op jit(solution)/shard_map/ppermute | solution.py:641
  269.5 2.3 copy-start.27
  269.5 45.6 %copy-start.25 = (f32[8,512]{1,0:T(8,128)S(1)}, f32[8,512]{1,0:T(8,128)}, u32[]{:S(2)}) copy-start(f32[8,512]{1,0:T(8,128)} %get-tuple-element.116) | copy-start | bytes 49156
  269.5 45.6 %copy-start.26 = (f32[8,512]{1,0:T(8,128)S(1)}, f32[8,512]{1,0:T(8,128)}, u32[]{:S(2)}) copy-start(f32[8,512]{1,0:T(8,128)} %get-tuple-element.115) | copy-start | bytes 49156
  271.3 91.9 %collective-permute-start.9 = (f32[1024,512]{1,0:T(8,128)}, f32[1024,512]{1,0:T(8,128)}, u32[]{:S(2)}, u32[]{:S(2)}) collective-permute-start(f32[1024,512]{1,0:T(8,128)} %broadcast_select_fusion.8), channel_id=1, source_target_pairs={{0,16},{16,0},{1,17},{17,1},{2,18},{18,2},{3,19},{19,3},{4,20},{20... | collective-permute-start | bytes 6291464 | tf_op jit(solution)/shard_map/ppermute | solution.py:641
  315.1 1.2 collective-permute-start.15
  360.6 2.6 copy-start.4
  360.6 3.8 copy-start.6
  408.2 197.6 %copy-start.24 = (bf16[1,512,512]{2,1,0:T(8,128)(2,1)S(1)}, bf16[1,512,512]{2,1,0:T(8,128)(2,1)}, u32[]{:S(2)}) copy-start(bf16[1,512,512]{2,1,0:T(8,128)(2,1)} %get-tuple-element.128) | copy-start | bytes 1572868
  604.6 2.9 copy-start.21
  604.6 2.9 copy-start.22
  607.4 2.4 copy-start.19
  607.4 3.7 copy-start.20
  611.2 2.4 copy-start.1
Sparse Core Ops, SparseCore 0:
  264.4 141.6 all-reduce.7
  412.5 191.9 all-reduce.5
